TPU v7x, 128 devices: a whole 4x4x4 slice. The times are simulated.
128 devices in a mesh: layer: 4 (over z), tile: 32 (over x, y, core).
Axes of the slice: x: 4, y: 4, z: 4, core: 2. Of those that a mesh axis runs over, the one named last changes fastest.
Arguments:
- leaf_rhs: float32 [4, 128, 128, 256], P('layer', 'tile'), may hold values from -6 to 6
- leaf_inv: float32 [4, 128, 128, 128], P('layer', 'tile'), as said below
- par_rhs: float32 [4, 64, 128, 256], P('layer', 'tile'), may hold values from -6 to 6
- par_inv: float32 [4, 64, 128, 128], P('layer', 'tile'), as said below
- top_rhs: float32 [64, 128, 256], P('tile', None, 'layer'), may hold values from -6 to 6
- top_inv: float32 [64, 128, 128], P('tile'), as said below
- leaf_tiles: float32 [4, 5120, 128, 128], P('layer', 'tile'), may hold values from -0.125 to 0.125
- leaf_cols: int32 [4, 5120], P('layer', 'tile'), may hold values from 0 to 3
- leaf_rows: int32 [4, 5120], P('layer', 'tile'), may hold values from 0 to 127, as said below
- leaf_count: int32 [4, 32], P('layer', 'tile'), may hold values from 1 to 160, as said below
- par_tiles: float32 [4, 2560, 128, 128], P('layer', 'tile'), may hold values from -0.125 to 0.125
- par_cols: int32 [4, 2560], P('layer', 'tile'), may hold values from 0 to 1
- par_rows: int32 [4, 2560], P('layer', 'tile'), may hold values from 0 to 63
- par_count: int32 [4, 32], P('layer', 'tile'), may hold values from 1 to 80, as said below
Outputs:
- parent_solution: float32 [4, 64, 128, 256], P('layer', 'tile')
- top_solution: float32 [64, 128, 256], P('tile', None, 'layer')
Inputs may be any that keep to these rules, and one draw needn't show every extreme that they name: `leaf_inv`: lower triangular, diagonal entries of magnitude 0.5 to 2. `par_inv`: lower triangular, diagonal entries of magnitude 0.5 to 2. `top_inv`: lower triangular, diagonal entries of magnitude 0.5 to 2. `leaf_rows`: the elimination subtree of a lower-level supernode of owner o lies in o's group of owners: owners o and q share a group when o // 2 % (4) equals q // 2 % 4; a tile below 64 names an upper-level supernode held by an owner of the same group, and the top-level supernodes are ancestors of every subtree. `leaf_count`: some owner of every layer has a full list. `par_count`: some owner of every layer has a full list.
All inputs are finite; a program needn't handle non-finite values.
Results may differ from a plain program's by a relative error of at most 0.0003.
Values sent between devices are 32-bit elements; how exact they have to be, the bound alone decides.
A program may use at most 128 MiB of HBM per device.

v0:
```python
import jax
import jax.numpy as jnp
from jax import lax
from jax.sharding import PartitionSpec as P


def tile_products(tiles, cols, count, solved):
    highest = lax.Precision.HIGHEST
    picked = jnp.take(solved, cols, axis=0)
    product = jnp.einsum("tij,tjk->tik", tiles, picked, precision=highest)
    slots = tiles.shape[0]
    in_use = jnp.arange(slots, dtype=jnp.int32) < count
    return (product.reshape(slots, -1), in_use)


def collect(targets_of, in_use, products, first, number):
    highest = lax.Precision.HIGHEST
    wanted = first + jnp.arange(number, dtype=jnp.int32)
    selector = jnp.logical_and(targets_of[None, :] == wanted[:, None], in_use[None, :]).astype(
        jnp.float32
    )
    return jnp.dot(selector, products, precision=highest, preferred_element_type=jnp.float32)


def local(
    leaf_rhs,
    leaf_inv,
    par_rhs,
    par_inv,
    top_rhs,
    top_inv,
    leaf_tiles,
    leaf_cols,
    leaf_rows,
    leaf_count,
    par_tiles,
    par_cols,
    par_rows,
    par_count,
):
    highest = lax.Precision.HIGHEST
    block = leaf_rhs.shape[2]
    columns = leaf_rhs.shape[3]
    owners = lax.axis_size("tile")
    parent_here = par_rhs.shape[1]
    parent_total = parent_here * owners
    top_total = top_inv.shape[0] * owners
    leaf_solution = jnp.einsum("bij,bjk->bik", leaf_inv[0], leaf_rhs[0], precision=highest)
    leaf_products, leaf_used = tile_products(
        leaf_tiles[0], leaf_cols[0], leaf_count[0, 0], leaf_solution
    )
    leaf_targets = leaf_rows[0]
    summed = collect(
        leaf_targets, leaf_used, leaf_products, jnp.int32(0), parent_here * lax.axis_size("tile")
    )
    parent_sum = lax.psum_scatter(
        summed.reshape(parent_here * lax.axis_size("tile"), block, columns),
        "tile",
        scatter_dimension=0,
        tiled=True,
    )
    parent_solution = jnp.einsum(
        "bij,bjk->bik", par_inv[0], par_rhs[0] - parent_sum, precision=highest
    )
    par_products, par_used = tile_products(
        par_tiles[0], par_cols[0], par_count[0, 0], parent_solution
    )
    top_local = collect(leaf_targets, leaf_used, leaf_products, parent_total, top_total)
    top_local = top_local + collect(par_rows[0], par_used, par_products, 0, top_total)
    top_local = top_local.reshape(top_total, block, columns)
    owned_rows = lax.psum_scatter(top_local, "tile", scatter_dimension=0, tiled=True)
    owned = lax.psum_scatter(owned_rows, "layer", scatter_dimension=2, tiled=True)
    top_solution = jnp.einsum("bij,bjk->bik", top_inv, top_rhs - owned, precision=highest)
    return (parent_solution[None], top_solution)


def solution(mesh):
    in_specs = (
        P("layer", "tile", None, None),
        P("layer", "tile", None, None),
        P("layer", "tile", None, None),
        P("layer", "tile", None, None),
        P("tile", None, "layer"),
        P("tile", None, None),
        P("layer", "tile", None, None),
        P("layer", "tile"),
        P("layer", "tile"),
        P("layer", "tile"),
        P("layer", "tile", None, None),
        P("layer", "tile"),
        P("layer", "tile"),
        P("layer", "tile"),
    )
    out_specs = (P("layer", "tile", None, None), P("tile", None, "layer"))
    return jax.shard_map(local, mesh=mesh, in_specs=in_specs, out_specs=out_specs, check_vma=False)
```

profile of v0, /device:TPU:0, one launch (start us, length us, event | category | flops | bytes accessed | tf_op | source)
XLA Modules:
  0.0 384.4 jit_solution(3432063577769573596)
XLA Ops:
  7.2 0.0 copy-start
  7.2 0.0 reduce-scatter.4.cloned.1.call-start
  7.9 0.7 compare_select_fusion
  8.6 0.7 compare_and_fusion.1
  9.3 1.5 fusion.23
  10.9 8.6 %gather_fusion = f32[160,128,256]{2,1,0:T(8,128)} fusion(f32[4,128,256]{2,1,0:T(8,128)S(1)} %fusion.23, s32[1024]{0:T(1024)S(1)} %pad_clamp_fusion.1), kind=kCustom, calls=%fused_computation | custom fusion | bytes 41943680 | tf_op jit(solution)/shard_map/jit(_take)/gather | solution.py:9
  19.5 42.0 %fusion.10 = f32[160,128,256]{1,2,0:T(8,128)} fusion(f32[1,160,128,128]{3,2,1,0:T(8,128)} %param.20, f32[160,128,256]{2,1,0:T(8,128)} %gather_fusion, pred[160]{0:T(512)(128)(4,1)S(1)} %compare_and_fusion.1), kind=kOutput, calls=%fused_computation.13 | convolution fusion | flops 8058306560 | bytes 52428960 | tf_op jit(solution)/shard_map/tij,tjk->tik/dot_general | solution.py:10
  61.4 21.3 %copy.30 = f32[20,8,128,256]{3,1,2,0:T(8,128)} copy(f32[20,8,128,256]{2,3,1,0:T(8,128)} %bitcast.73) | data formatting | bytes 41943040
  82.8 13.4 %fusion = f32[64,128,256]{2,0,1:T(8,128)S(1)} fusion(s32[160]{0:T(256)S(1)} %bitcast.78, pred[160]{0:T(512)(128)(4,1)S(1)} %iota_compare_fusion.2, f32[20,8,128,256]{3,1,2,0:T(8,128)} %copy.30), kind=kOutput, calls=%fused_computation.3 | convolution fusion | flops 4026552320 | bytes 29360928 | tf_op jit(solution)/shard_map/dot_general | solution.py:22
  96.1 0.0 copy-start.8
  96.2 8.2 %copy.27 = f32[64,128,256]{2,1,0:T(8,128)} copy(f32[64,128,256]{2,0,1:T(8,128)S(1)} %fusion) | data formatting | bytes 16777216 | tf_op jit(solution)/shard_map/dot_general | solution.py:22
  104.4 0.0 reduce-scatter.4.cloned.1.call-update
  104.4 0.0 reduce-scatter.6.cloned.1.call-start
  105.1 0.0 copy-done.8
  105.2 0.0 copy-start.2
  105.2 0.0 copy-start.3
  105.2 14.6 %fusion.32 = f32[64,32768]{1,0:T(8,128)} fusion(f32[160,32768]{1,0:T(8,128)} %bitcast.72, s32[160]{0:T(256)S(1)} %bitcast.79, s32[64]{0:T(128)S(1)} %iota_add_fusion, pred[160]{0:T(512)(128)(4,1)S(1)} %iota_compare_fusion.2), kind=kOutput, calls=%fused_computation.29 | convolution fusion | flops 4026552320 | bytes 29361184 | tf_op jit(solution)/shard_map/dot_general | solution.py:22
  119.8 79.8 %reduce-scatter.4.cloned.1.call-done = f32[2,128,256]{2,1,0:T(8,128)} async-done(((f32[64,128,256]{2,1,0:T(8,128)}), f32[2,128,256]{2,1,0:T(8,128)}) %reduce-scatter.4.cloned.1.call-update) | async-done | bytes 262160 | tf_op jit(solution)/shard_map/reduce_scatter | solution.py:56
  199.6 1.5 fusion.26
  201.2 5.0 %gather_fusion.1 = f32[80,128,256]{1,2,0:T(8,128)} fusion(f32[2,128,256]{1,2,0:T(8,128)S(1)} %bitcast.70, s32[1024]{0:T(1024)S(1)} %pad_clamp_fusion), kind=kCustom, calls=%fused_computation.1 | custom fusion | bytes 20971840 | tf_op jit(solution)/shard_map/jit(_take)/gather | solution.py:9
  206.2 14.9 %fusion.18 = f32[80,128,256]{1,2,0:T(8,128)} fusion(f32[1,80,128,128]{3,2,1,0:T(8,128)} %param.24, f32[80,128,256]{1,2,0:T(8,128)} %gather_fusion.1, pred[80]{0:T(512)(128)(4,1)S(1)} %compare_and_fusion), kind=kOutput, calls=%fused_computation.17 | convolution fusion | flops 4029153280 | bytes 26214480 | tf_op jit(solution)/shard_map/tij,tjk->tik/dot_general | solution.py:10
  221.1 11.8 %copy.31 = f32[10,8,128,256]{3,1,2,0:T(8,128)} copy(f32[10,8,128,256]{2,3,1,0:T(8,128)} %bitcast.74) | data formatting | bytes 20971520
  232.9 13.1 %convolution_add_fusion = f32[64,32768]{1,0:T(8,128)S(1)} fusion(f32[64,32768]{1,0:T(8,128)} %fusion.32, f32[80,32768]{1,0:T(8,128)} %bitcast.75, s32[80]{0:T(128)S(1)} %bitcast.82, pred[80]{0:T(512)(128)(4,1)S(1)} %iota_compare_fusion.3), kind=kOutput, calls=%fused_computation.2 | convolution fusion | flops 2015373312 | bytes 27263376 | tf_op jit(solution)/shard_map/dot_general | solution.py:22
  246.0 5.7 %copy.32 = f32[8,8,128,256]{3,2,1,0:T(8,128)} copy(f32[8,8,128,256]{3,1,2,0:T(8,128)S(1)} %bitcast.77) | data formatting | bytes 16777216
  251.7 9.1 %copy.23 = f32[64,128,256]{1,2,0:T(8,128)} copy(f32[64,128,256]{2,1,0:T(8,128)} %bitcast.76) | data formatting | bytes 16777216 | tf_op jit(solution)/shard_map/reshape | solution.py:70
  260.8 0.0 reduce-scatter.6.cloned.1.call-update
  260.8 0.0 reduce-scatter.8.cloned.1.call-start
  260.9 92.1 %reduce-scatter.6.cloned.1.call-done = f32[2,128,256]{1,2,0:T(8,128)} async-done(((f32[64,128,256]{1,2,0:T(8,128)}), f32[2,128,256]{1,2,0:T(8,128)}) %reduce-scatter.6.cloned.1.call-update) | async-done | bytes 262160 | tf_op jit(solution)/shard_map/reduce_scatter | solution.py:71
  352.9 0.0 reduce-scatter.8.cloned.1.call-update
  353.0 0.8 copy.24
  353.8 21.8 %reduce-scatter.8.cloned.1.call-done = f32[2,128,64]{1,2,0:T(8,128)} async-done(((f32[2,128,256]{1,2,0:T(8,128)}), f32[2,128,64]{1,2,0:T(8,128)}) %reduce-scatter.8.cloned.1.call-update) | async-done | bytes 65552 | tf_op jit(solution)/shard_map/reduce_scatter | solution.py:72
  375.6 1.8 convolution_bitcast_fusion
  (20 shorter events, 0.1 us)
Async XLA Ops:
  7.2 2.2 copy-start
  7.2 192.4 %reduce-scatter.4.cloned.1.call-start = ((), (), s32[]{:S(2)}) async-start(), calls=%async_computation.3 | async-start | bytes 8650752 | tf_op jit(solution)/shard_map/reduce_scatter | solution.py:56
  61.4 21.3 %copy-start.6 = (s32[1,160]{1,0:T(1,128)S(1)}, s32[1,160]{1,0:T(1,128)}, u32[]{:S(2)}) copy-start(s32[1,160]{1,0:T(1,128)} %param.22) | copy-start | bytes 1924
  96.1 9.0 %copy-start.8 = (s32[1,80]{1,0:T(1,128)S(1)}, s32[1,80]{1,0:T(1,128)}, u32[]{:S(2)}) copy-start(s32[1,80]{1,0:T(1,128)} %param.25) | copy-start | bytes 964
  104.4 248.5 %reduce-scatter.6.cloned.1.call-start = ((), (), s32[]{:S(2)}) async-start(), calls=%async_computation.4 | async-start | bytes 8650752 | tf_op jit(solution)/shard_map/reduce_scatter | solution.py:71
  105.2 94.4 %copy-start.2 = (f32[1,2,128,256]{3,2,1,0:T(8,128)S(1)}, f32[1,2,128,256]{3,2,1,0:T(8,128)}, u32[]{:S(2)}) copy-start(f32[1,2,128,256]{3,2,1,0:T(8,128)} %param.16) | copy-start | bytes 786436
  105.2 94.4 %copy-start.3 = (f32[1,2,128,128]{3,2,1,0:T(8,128)S(1)}, f32[1,2,128,128]{3,2,1,0:T(8,128)}, u32[]{:S(2)}) copy-start(f32[1,2,128,128]{3,2,1,0:T(8,128)} %param.17) | copy-start | bytes 393220
  221.1 11.8 %copy-start.7 = (s32[1,80]{1,0:T(1,128)S(1)}, s32[1,80]{1,0:T(1,128)}, u32[]{:S(2)}) copy-start(s32[1,80]{1,0:T(1,128)} %param.26) | copy-start | bytes 964
  251.7 125.7 %copy-start.1 = (f32[1,4,128,256]{3,2,1,0:T(8,128)S(1)}, f32[1,4,128,256]{3,2,1,0:T(8,128)}, u32[]{:S(2)}) copy-start(f32[1,4,128,256]{3,2,1,0:T(8,128)} %param.14) | copy-start | bytes 1572868
  251.7 123.9 %copy-start.4 = (f32[2,128,128]{2,1,0:T(8,128)S(1)}, f32[2,128,128]{2,1,0:T(8,128)}, u32[]{:S(2)}) copy-start(f32[2,128,128]{2,1,0:T(8,128)} %param.19) | copy-start | bytes 393220
  251.7 123.9 %copy-start.5 = (f32[2,128,64]{1,2,0:T(8,128)S(1)}, f32[2,128,64]{1,2,0:T(8,128)}, u32[]{:S(2)}) copy-start(f32[2,128,64]{1,2,0:T(8,128)} %param.18) | copy-start | bytes 196612
  260.8 114.8 %reduce-scatter.8.cloned.1.call-start = ((), (), s32[]{:S(2)}) async-start(), calls=%async_computation.5 | async-start | bytes 327680 | tf_op jit(solution)/shard_map/reduce_scatter | solution.py:72
Sparse Core Ops, SparseCore 0:
  104.5 95.0 reduce-scatter.3
  260.9 91.9 reduce-scatter.5
  355.3 20.2 reduce-scatter.7
where the time goes:
time: 392 us; the launch traced here: 384 us
  waiting for transfers between devices  194 us (49%)
  matrix products  103 us (26%)
  local copies, waits for them, and re-layouts  70.7 us (18%)
  between operations  15.7 us (4%)
    reduce_scatter x1, waiting for transfers between devices, local(): lax.psum_scatter(top_local, 'tile', scatter_dimension=0, tiled=True)  92.1 us
    reduce_scatter x1, waiting for transfers between devices, local(): lax.psum_scatter(summed.reshape(parent_here * lax.axis_size('tile'), bloc...  79.8 us
    dot_general x2, matrix products, tile_products(): product = jnp.einsum('tij,tjk->tik', tiles, picked, precision=highest)  56.8 us
    dot_general x3, matrix products, collect(): jnp.dot(selector, products, precision=highest, preferred_element_type=jnp...  41 us
    unnamed x22, local copies, waits for them, and re-layouts  39.8 us
    reduce_scatter x1, waiting for transfers between devices, local(): lax.psum_scatter(owned_rows, 'layer', scatter_dimension=2, tiled=True)  21.8 us
    gather x2, local copies, waits for them, and re-layouts, tile_products(): picked = jnp.take(solved, cols, axis=0)  13.7 us
    reshape x1, local copies, waits for them, and re-layouts, local(): top_local = top_local.reshape(top_total, block, columns)  9.07 us
  transfers between devices with their start and end apart: 3, of which 3 were waited for; matrix products, arithmetic and copies ran while one was open for 4% of the time, Pallas kernels for 0%

commit v1 on v0

v1 whole, which is shorter than its diff:
```python
import jax
import jax.numpy as jnp
from jax import lax
from jax.experimental import pallas as pl
from jax.experimental.pallas import tpu as pltpu
from jax.sharding import PartitionSpec as P

MESH = pl.DeviceIdType.MESH
F32, BF16 = jnp.float32, jnp.bfloat16
BS, NR = 128, 256
CH = 16
UN = 4
ROWS = ((0, 48), (48, 40), (88, 40))
VMEM_LIMIT = 56 * 2**20


def split(t):
    hi = t.astype(BF16)
    return hi, (t - hi.astype(F32)).astype(BF16)


def lhs_cat(t):
    hi, lo = split(t)
    return jnp.concatenate([hi, lo, hi], axis=1)


def rhs_cat(t):
    hi, lo = split(t)
    return jnp.concatenate([hi, hi, lo], axis=0)


def local_kernel(
    lrow, lcol, lcnt, prow, pcol, pcnt, rhs, inv, ltiles, ptiles,
    g_out, l_out, v_out,
    xw, acc, vacc, lt, pt, lsem, psem, osem,
):
    nl, npar = lt.shape[0], pt.shape[0]
    count, pcount = lcnt[0, 0], pcnt[0, 0]

    def chunk(src, dst, sem, i):
        return pltpu.make_async_copy(src.at[pl.ds(i * CH, CH)], dst.at[pl.ds(i * CH, CH)], sem.at[i])

    for i in range(nl // CH):
        @pl.when(i * CH < count)
        def _():
            chunk(ltiles, lt, lsem, i).start()
    for i in range(npar // CH):
        @pl.when(i * CH < pcount)
        def _():
            chunk(ptiles, pt, psem, i).start()

    for c in range(4):
        x = jnp.dot(inv[c], rhs[c], precision=lax.Precision.HIGHEST, preferred_element_type=F32)
        xw[c] = rhs_cat(x)

    @pl.loop(0, acc.shape[0])
    def _(i):
        acc[i] = jnp.zeros((BS, NR), F32)

    @pl.loop(0, vacc.shape[0])
    def _(i):
        vacc[i] = jnp.zeros((2, BS, BS), F32)

    dummy = acc.shape[0] - 1

    def group(g, _):
        @pl.when(lax.rem(g, CH // UN) == 0)
        def _():
            chunk(ltiles, lt, lsem, g // (CH // UN)).wait()

        where, prods = [], []
        for u in range(UN):
            s = g * UN + u
            r = lrow[0, s]
            par = ((r >> 1) & 1) * 8 + (r >> 4) * 2 + (r & 1)
            t = r - 64
            top = 16 + ((t >> 1) & 1) * 32 + (t >> 2) * 2 + (t & 1)
            idx = jnp.where(r < 64, par, top)
            where.append(jnp.where(s < count, idx, dummy))
            prods.append(jnp.dot(lhs_cat(lt[s]), xw[lcol[0, s]], preferred_element_type=F32))
        for u in range(UN):
            acc[where[u]] += prods[u]
        return 0

    lax.fori_loop(0, (count + UN - 1) // UN, group, 0)
    g_copy = pltpu.make_async_copy(acc.at[pl.ds(0, 16)], g_out, osem.at[0])
    l_copy = pltpu.make_async_copy(acc.at[pl.ds(16, 64)], l_out, osem.at[1])
    g_copy.start()
    l_copy.start()

    def dense(s, _):
        @pl.when(lax.rem(s, CH) == 0)
        def _():
            chunk(ptiles, pt, psem, s // CH).wait()

        t = prow[0, s]
        top = ((t >> 1) & 1) * 32 + (t >> 2) * 2 + (t & 1)
        vacc[top, pcol[0, s]] += pt[s]
        return 0

    lax.fori_loop(0, pcount, dense, 0)
    v_copy = pltpu.make_async_copy(vacc, v_out, osem.at[2])
    v_copy.start()
    g_copy.wait()
    l_copy.wait()
    v_copy.wait()


def main_kernel(
    par_inv, par_rhs, top_inv, top_rhs, g, l, v,
    psol, tsol,
    g_own, g_sib, g_send, g_two, g_prev, g_next, x_own, x_sib, xw,
    l_own, l_sib, v_own, v_sib,
    d, e, f, h, two, prev, nxt, total,
    loc, sib_s, sib_r, gs, gr, rs_s, rs_r,
):
    z = lax.axis_index("layer")
    tile = lax.axis_index("tile")
    x, y, c = tile // 8, (tile // 2) % 4, tile % 2
    pos = (x, y, z)

    def at(axis, step):
        q = [x, y, z]
        q[axis] = (q[axis] + step + 4) % 4
        return (q[2], q[0] * 8 + q[1] * 2 + c)

    sib = (z, x * 8 + y * 2 + 1 - c)
    barrier = pltpu.get_barrier_semaphore()
    peers = [sib] + [at(a, s) for a in range(3) for s in (1, -1)]
    for p in peers:
        pl.semaphore_signal(barrier, inc=1, device_id=p, device_id_type=MESH)

    own = [
        pltpu.make_async_copy(g.at[c], g_own, loc.at[0]),
        pltpu.make_async_copy(v.at[c], v_own, loc.at[1]),
        pltpu.make_async_copy(l.at[c], l_own, loc.at[2]),
    ]
    for copy in own:
        copy.start()
    pl.semaphore_wait(barrier, len(peers))

    started = []

    def send(src, dst, ssem, rsem, device):
        copy = pltpu.make_async_remote_copy(
            src_ref=src, dst_ref=dst, send_sem=ssem, recv_sem=rsem, device_id=device, device_id_type=MESH
        )
        copy.start()
        started.append(copy)
        return copy

    order = [(x + 2) % 4, (x + 1) % 4, (x + 3) % 4, x]
    swap = [send(g.at[1 - c, q], g_sib.at[q], sib_s.at[i], sib_r.at[i], sib) for i, q in enumerate(order)]
    v_swap = send(v.at[1 - c], v_sib, sib_s.at[4], sib_r.at[4], sib)
    l_swap = send(l.at[1 - c], l_sib, sib_s.at[5], sib_r.at[5], sib)

    own[0].wait()
    right, left = at(0, 1), at(0, -1)
    for i in range(3):
        swap[i].wait_recv()
        g_send[i] = g_own[order[i]] + g_sib[order[i]]
        if i == 0:
            a2 = send(g_send.at[0, 0], g_two.at[0], gs.at[0], gr.at[0], right)
            b2 = send(g_send.at[0, 1], g_two.at[1], gs.at[1], gr.at[1], left)
        elif i == 1:
            p1 = send(g_send.at[1, 1], g_prev.at[1], gs.at[2], gr.at[2], right)
        else:
            n0 = send(g_send.at[2, 0], g_next.at[0], gs.at[3], gr.at[3], left)
    a2.wait_recv()
    g_send[1, 0] = g_send[1, 0] + g_two[0]
    p0 = send(g_send.at[1, 0], g_prev.at[0], gs.at[4], gr.at[4], right)
    b2.wait_recv()
    g_send[2, 1] = g_send[2, 1] + g_two[1]
    n1 = send(g_send.at[2, 1], g_next.at[1], gs.at[5], gr.at[5], left)
    swap[3].wait_recv()
    for copy in (p1, n0, p0, n1):
        copy.wait_recv()
    for j in range(2):
        update = g_own[x, j] + g_sib[x, j] + g_prev[j] + g_next[j]
        solved = jnp.dot(
            par_inv[j], par_rhs[j] - update, precision=lax.Precision.HIGHEST, preferred_element_type=F32
        )
        x_own[pl.ds(j * BS, BS)] = solved
        psol[j] = solved
    x_swap = send(x_own, x_sib, sib_s.at[6], sib_r.at[6], sib)
    xw[0] = rhs_cat(x_own[...])
    x_swap.wait_recv()
    xw[1] = rhs_cat(x_sib[...])
    own[1].wait()
    own[2].wait()
    v_swap.wait_recv()
    l_swap.wait_recv()

    low = lax.broadcasted_iota(jnp.int32, (BS, BS), 1) < 64

    @pl.loop(0, 16)
    def _(k):
        kx, ky = k // 4, k % 4
        sums = []
        for j in range(2):
            left_own = lhs_cat(jnp.concatenate([v_own[k, j, 0], v_own[k, j, 1]], axis=1))
            left_sib = lhs_cat(jnp.concatenate([v_sib[k, j, 0], v_sib[k, j, 1]], axis=1))
            sums.append(
                l_own[k, j] + l_sib[k, j]
                + jnp.dot(left_own, xw[0], preferred_element_type=F32)
                + jnp.dot(left_sib, xw[1], preferred_element_type=F32)
            )
        for half in range(2):
            first = sums[0][:, half * BS:(half + 1) * BS]
            second = pltpu.roll(sums[1][:, half * BS:(half + 1) * BS], 64, 1)
            for odd in range(2):
                q = jnp.where(low, second, first) if odd else jnp.where(low, first, second)
                kz = half * 2 + odd
                for p, spot in enumerate(((kx, ky, kz), (ky, kz, kx), (kz, kx, ky))):
                    d[p][spot[0], spot[1], spot[2]] = q[ROWS[p][0]:ROWS[p][0] + ROWS[p][1]]

    source = [d, e, f]
    target = [e, f, h]
    flying = {}

    def halves(p, ph):
        if ph < 2:
            return pl.ds(0, 2), pl.ds(2, 2)
        n = ROWS[p][1]
        a = (n // 16) * 8 + (8 if n % 16 else 0)
        return pl.ds(0, a), pl.ds(a, n - a)

    def issue(p, ph):
        axis = (p + ph) % 3
        m = pos[axis]
        src = source[ph][p]
        a, b = halves(p, ph)
        fwd, bwd = at(axis, 1), at(axis, -1)
        ss, rr = rs_s.at[p, ph], rs_r.at[p, ph]
        far, up, down = (m + 2) % 4, (m + 1) % 4, (m + 3) % 4
        flying[p, ph] = [
            send(src.at[far, a], two[ph][p].at[a], ss.at[0], rr.at[0], fwd),
            send(src.at[far, b], two[ph][p].at[b], ss.at[1], rr.at[1], bwd),
            send(src.at[up, b], prev[ph][p].at[b], ss.at[2], rr.at[2], fwd),
            send(src.at[down, a], nxt[ph][p].at[a], ss.at[3], rr.at[3], bwd),
        ]

    def middle(p, ph):
        axis = (p + ph) % 3
        m = pos[axis]
        src = source[ph][p]
        a, b = halves(p, ph)
        ss, rr = rs_s.at[p, ph], rs_r.at[p, ph]
        up, down = (m + 1) % 4, (m + 3) % 4
        copies = flying[p, ph]
        copies[0].wait_recv()
        src[up, a] = src[up, a] + two[ph][p][a]
        copies.append(send(src.at[up, a], prev[ph][p].at[a], ss.at[4], rr.at[4], at(axis, 1)))
        copies[1].wait_recv()
        src[down, b] = src[down, b] + two[ph][p][b]
        copies.append(send(src.at[down, b], nxt[ph][p].at[b], ss.at[5], rr.at[5], at(axis, -1)))

    def finish(p, ph):
        m = pos[(p + ph) % 3]
        for copy in flying[p, ph][2:]:
            copy.wait_recv()
        target[ph][p][...] = source[ph][p][m] + prev[ph][p][...] + nxt[ph][p][...]

    for p in range(3):
        issue(p, 0)
    for ph in range(3):
        for p in range(3):
            middle(p, ph)
        for p in range(3):
            finish(p, ph)
            if ph < 2:
                issue(p, ph + 1)

    for p in range(3):
        total[pl.ds(*ROWS[p])] = h[p][...]
    turned = pltpu.roll(total[...], 64, 1)
    odd = z % 2 == 1
    ancestor = (jnp.where(odd, turned, total[...]), jnp.where(odd, total[...], turned))
    for j in range(2):
        tsol[j] = jnp.dot(
            top_inv[j], top_rhs[j] - ancestor[j][:, :64], precision=lax.Precision.HIGHEST,
            preferred_element_type=F32,
        )
    for copy in started:
        copy.wait_send()


def local(
    leaf_rhs, leaf_inv, par_rhs, par_inv, top_rhs, top_inv, leaf_tiles, leaf_cols, leaf_rows, leaf_count,
    par_tiles, par_cols, par_rows, par_count,
):
    vm = pl.BlockSpec(memory_space=pltpu.VMEM)
    sm = pl.BlockSpec(memory_space=pltpu.SMEM)
    hb = pl.BlockSpec(memory_space=pl.ANY)
    nl, npar = leaf_tiles.shape[1], par_tiles.shape[1]
    shape = jax.ShapeDtypeStruct
    g, l, v = pl.pallas_call(
        local_kernel,
        out_shape=(
            shape((16, BS, NR), F32),
            shape((64, BS, NR), F32),
            shape((64, 2, BS, BS), F32),
        ),
        in_specs=[sm] * 6 + [vm, vm, hb, hb],
        out_specs=(hb, hb, hb),
        scratch_shapes=[
            pltpu.VMEM((4, 3 * BS, NR), BF16),
            pltpu.VMEM((81, BS, NR), F32),
            pltpu.VMEM((64, 2, BS, BS), F32),
            pltpu.VMEM((nl, BS, BS), F32),
            pltpu.VMEM((npar, BS, BS), F32),
            pltpu.SemaphoreType.DMA((nl // CH,)),
            pltpu.SemaphoreType.DMA((npar // CH,)),
            pltpu.SemaphoreType.DMA((3,)),
        ],
        compiler_params=pltpu.CompilerParams(vmem_limit_bytes=VMEM_LIMIT),
        name="leaf",
    )(leaf_rows, leaf_cols, leaf_count, par_rows, par_cols, par_count, leaf_rhs[0], leaf_inv[0], leaf_tiles[0], par_tiles[0])

    n = [r for _, r in ROWS]
    lead = ((4, 4), (4,), ())
    dma = pltpu.SemaphoreType.DMA

    def per_phase(extra):
        return [[pltpu.VMEM(extra + lead[ph] + (r, BS), F32) for r in n] for ph in range(3)]

    block = pltpu.VMEM((2, BS, NR), F32)
    psol, tsol = pl.pallas_call(
        main_kernel,
        out_shape=(shape((2, BS, NR), F32), shape((2, BS, 64), F32)),
        in_specs=[vm] * 4 + [hb] * 3,
        out_specs=(vm, vm),
        scratch_shapes=[
            pltpu.VMEM((4, 2, BS, NR), F32), pltpu.VMEM((4, 2, BS, NR), F32), pltpu.VMEM((3, 2, BS, NR), F32),
            block, block, block,
            pltpu.VMEM((2 * BS, NR), F32), pltpu.VMEM((2 * BS, NR), F32), pltpu.VMEM((2, 6 * BS, NR), BF16),
            pltpu.VMEM((16, 2, BS, NR), F32), pltpu.VMEM((16, 2, BS, NR), F32),
            pltpu.VMEM((16, 2, 2, BS, BS), F32), pltpu.VMEM((16, 2, 2, BS, BS), F32),
            [pltpu.VMEM((4, 4, 4, r, BS), F32) for r in n],
            [pltpu.VMEM((4, 4, r, BS), F32) for r in n],
            [pltpu.VMEM((4, r, BS), F32) for r in n],
            [pltpu.VMEM((r, BS), F32) for r in n],
            per_phase(()), per_phase(()), per_phase(()),
            pltpu.VMEM((BS, BS), F32),
            dma((3,)), dma((7,)), dma((7,)), dma((6,)), dma((6,)), dma((3, 3, 6)), dma((3, 3, 6)),
        ],
        compiler_params=pltpu.CompilerParams(
            collective_id=0, has_side_effects=True, vmem_limit_bytes=VMEM_LIMIT
        ),
        name="main",
    )(
        par_inv[0], par_rhs[0], top_inv, top_rhs,
        g.reshape(2, 4, 2, BS, NR), l.reshape(2, 16, 2, BS, NR), v.reshape(2, 16, 2, 2, BS, BS),
    )
    return psol[None], tsol


def solution(mesh):
    four = P("layer", "tile", None, None)
    pair = P("layer", "tile")
    top = P("tile", None, "layer")
    in_specs = (
        four, four, four, four, top, P("tile", None, None), four, pair, pair, pair, four, pair, pair, pair,
    )
    return jax.shard_map(local, mesh=mesh, in_specs=in_specs, out_specs=(four, top), check_vma=False)
```

time: 392 us -> 89.5 us (0.23); the launches traced: 384 us -> 89.2 us
  waiting for transfers between devices: 194 us -> 0 us
  matrix products: 103 us -> 0 us
  Pallas kernels: 0 us -> 82.4 us
  local copies, waits for them, and re-layouts: 70.7 us -> 4.88 us
  between operations: 15.7 us -> 1.94 us
    reduce_scatter x3 -> x0, waiting for transfers between devices: 194 us -> none  [the longest x1 92.1 us: local(): lax.psum_scatter(top_local, 'tile', scatter_dimension=0, tiled=True)]
    dot_general x8 -> x0, matrix products: 103 us -> none  [the longest x2 56.8 us: tile_products(): product = jnp.einsum('tij,tjk->tik', tiles, picked, precision=highest)]
    pallas_call x0 -> x2, Pallas kernels: none -> 82.4 us  [the longest x1 66.2 us: local(): pl.pallas_call(main_kernel, out_shape=(shape((2, BS, NR), F32), shape((2,...]
    unnamed x22 -> x3, local copies, waits for them, and re-layouts: 39.8 us -> 4.88 us
    gather x2 -> x0, local copies, waits for them, and re-layouts: 13.7 us -> none  [tile_products(): picked = jnp.take(solved, cols, axis=0)]
    reshape x1 -> x0, local copies, waits for them, and re-layouts: 9.07 us -> none  [local(): top_local = top_local.reshape(top_total, block, columns)]
    dot_general x1 -> x0, local copies, waits for them, and re-layouts: 8.21 us -> none  [collect(): jnp.dot(selector, products, precision=highest, preferred_element_type=jnp...]
  transfers between devices with their start and end apart: 3 -> 0, of which waited for: 3 -> 0; matrix products, arithmetic and copies ran while one was open for 4% -> 0% of each run, Pallas kernels for 0% -> 0%
where the time goes in v1:
time: 89.5 us; the launch traced here: 89.2 us
  Pallas kernels  82.4 us (92%)
  local copies, waits for them, and re-layouts  4.88 us (5%)
  between operations  1.94 us (2%)
    pallas_call x1, Pallas kernels, local(): pl.pallas_call(main_kernel, out_shape=(shape((2, BS, NR), F32), shape((2,...  66.2 us
    pallas_call x1, Pallas kernels, local(): pl.pallas_call(local_kernel, out_shape=(shape((16, BS, NR), F32), shape((...  16.2 us
    unnamed x3, local copies, waits for them, and re-layouts  4.88 us

profile of v1, /device:TPU:0, one launch (start us, length us, event | category | flops | bytes accessed | tf_op | source)
XLA Modules:
  0.0 89.2 jit_solution(14594098759367118821)
XLA Ops:
  1.9 1.6 %copy.16.top_rhs = f32[2,128,64]{2,1,0:T(8,128)} copy(f32[2,128,64]{1,2,0:T(8,128)} %param.18) | data formatting | bytes 131072 | tf_op args[4]
  3.5 16.2 %leaf.1 = (f32[16,128,256]{2,1,0:T(8,128)}, f32[64,128,256]{2,1,0:T(8,128)}, f32[64,2,128,128]{3,2,1,0:T(8,128)}) custom-call(s32[1,160]{1,0:T(1,128)} %lrow.1, s32[1,160]{1,0:T(1,128)} %lcol.1, s32[1,1]{1,0:T(1,128)S(6)} %copy.19.lcnt, s32[1,80]{1,0:T(1,128)} %prow.1, s32[1,80]{1,0:T(1,128)} %pcol.1, s32[1,1]{1,0:T(1,128)S(6)} %copy.20.pcnt, ...), custom_call_target="tpu_custom_call" | custom-call | tf_op jit(solution)/shard_map/leaf/pallas_call | solution.py:297
  19.7 66.2 %main.1 = (f32[2,128,256]{2,1,0:T(8,128)}, f32[2,128,64]{2,1,0:T(8,128)}) custom-call(f32[2,128,128]{2,1,0:T(8,128)} %bitcast.19, f32[2,128,256]{2,1,0:T(8,128)} %bitcast.17, f32[2,128,128]{2,1,0:T(8,128)} %top_inv.1, f32[2,128,64]{2,1,0:T(8,128)} %copy.16.top_rhs, f32[2,4,2,128,256]{4,3,2,1,0:T(8,128)} %bitcast.14, f32[2,16,2,128,256]{4,3,2,1,0:T(8,128)} %bitcast.11, ...), custom_call_target="tpu_custom_call" | custom-call | tf_op jit(solution)/shard_map/main/pallas_call | solution.py:328
  85.9 1.6 %copy.17 = f32[2,128,64]{1,2,0:T(8,128)} copy(f32[2,128,64]{2,1,0:T(8,128)} %get-tuple-element.13) | data formatting | bytes 131072
  87.5 1.7 %copy.21 = f32[1,2,128,256]{3,2,1,0:T(8,128)} copy(f32[1,2,128,256]{3,2,1,0:T(8,128)} %bitcast.18) | data formatting | bytes 524288

commit v2 on v1

v2 whole, which is shorter than its diff:
```python
import jax
import jax.numpy as jnp
from jax import lax
from jax.experimental import pallas as pl
from jax.experimental.pallas import tpu as pltpu
from jax.sharding import PartitionSpec as P

MESH = pl.DeviceIdType.MESH
F32, BF16 = jnp.float32, jnp.bfloat16
BS, NR = 128, 256
CH = 16
UN = 16
ROWS = ((0, 48), (48, 48), (96, 32))
DIRECT = (1, 2)


def split(t):
    hi = t.astype(BF16)
    return hi, (t - hi.astype(F32)).astype(BF16)


def lhs_cat(t):
    hi, lo = split(t)
    return jnp.concatenate([hi, lo, hi], axis=1)


def rhs_cat(t):
    hi, lo = split(t)
    return jnp.concatenate([hi, hi, lo], axis=0)


def local_kernel(
    lrow, lcol, lcnt, prow, pcol, pcnt, rhs, inv, ltiles, ptiles,
    acc, vacc,
    xw, lt, pt, lsem, psem,
):
    nl, npar = lt.shape[0], pt.shape[0]
    count, pcount = lcnt[0, 0], pcnt[0, 0]

    def chunk(src, dst, sem, i):
        return pltpu.make_async_copy(src.at[pl.ds(i * CH, CH)], dst.at[pl.ds(i * CH, CH)], sem.at[i])

    for i in range(nl // CH):
        @pl.when(i * CH < count)
        def _():
            chunk(ltiles, lt, lsem, i).start()
    for i in range(npar // CH):
        @pl.when(i * CH < pcount)
        def _():
            chunk(ptiles, pt, psem, i).start()

    for c in range(4):
        x = jnp.dot(inv[c], rhs[c], precision=lax.Precision.HIGHEST, preferred_element_type=F32)
        xw[c] = rhs_cat(x)

    @pl.loop(0, acc.shape[0])
    def _(i):
        acc[i] = jnp.zeros((BS, NR), F32)

    @pl.loop(0, vacc.shape[0])
    def _(i):
        vacc[i] = jnp.zeros((2, BS, BS), F32)

    dummy = acc.shape[0] - 1

    def group(g, _):
        @pl.when(lax.rem(g, CH // UN) == 0)
        def _():
            chunk(ltiles, lt, lsem, g // (CH // UN)).wait()

        where, prods = [], []
        for u in range(UN):
            s = g * UN + u
            r = lrow[0, s]
            par = ((r >> 1) & 1) * 8 + (r >> 4) * 2 + (r & 1)
            t = r - 64
            top = 16 + ((t >> 1) & 1) * 32 + (t >> 2) * 2 + (t & 1)
            idx = jnp.where(r < 64, par, top)
            where.append(jnp.where(s < count, idx, dummy))
            prods.append(jnp.dot(lhs_cat(lt[s]), xw[lcol[0, s]], preferred_element_type=F32))
        for u in range(UN):
            acc[where[u]] += prods[u]
        return 0

    lax.fori_loop(0, (count + UN - 1) // UN, group, 0)
    def dense(s, _):
        @pl.when(lax.rem(s, CH) == 0)
        def _():
            chunk(ptiles, pt, psem, s // CH).wait()

        t = prow[0, s]
        top = ((t >> 1) & 1) * 32 + (t >> 2) * 2 + (t & 1)
        vacc[top, pcol[0, s]] += pt[s]
        return 0

    lax.fori_loop(0, pcount, dense, 0)


def main_kernel(
    par_inv, par_rhs, acc, v,
    x_own, total,
    g_sib, g_send, g_two, g_prev, g_next, x_sib, xw,
    l_sib, v_sib, vh, vl,
    d, e, f, h, two, prev, nxt,
    sib_s, sib_r, gs, gr, rs_s, rs_r,
):
    z = lax.axis_index("layer")
    tile = lax.axis_index("tile")
    x, y, c = tile // 8, (tile // 2) % 4, tile % 2
    pos = (x, y, z)

    def at(axis, step):
        q = [x, y, z]
        q[axis] = (q[axis] + step + 4) % 4
        return (q[2], q[0] * 8 + q[1] * 2 + c)

    sib = (z, x * 8 + y * 2 + 1 - c)
    barrier = pltpu.get_barrier_semaphore()
    peers = [sib] + [at(a, s) for a in range(3) for s in (1, -1, 2)]
    for p in peers:
        pl.semaphore_signal(barrier, inc=1, device_id=p, device_id_type=MESH)

    def split_v(src, base, side):
        @pl.loop(0, 16)
        def _(k):
            for j in range(2):
                for b in range(2):
                    hi, lo = split(src[base + k * 2 + j, b])
                    vh[side, k, j, :, b * BS:(b + 1) * BS] = hi
                    vl[side, k, j, :, b * BS:(b + 1) * BS] = lo

    split_v(v, c * 32, 0)
    pl.semaphore_wait(barrier, len(peers))

    started = []

    def send(src, dst, ssem, rsem, device):
        copy = pltpu.make_async_remote_copy(
            src_ref=src, dst_ref=dst, send_sem=ssem, recv_sem=rsem, device_id=device, device_id_type=MESH
        )
        copy.start()
        started.append(copy)
        return copy

    order = [(x + 2) % 4, (x + 1) % 4, (x + 3) % 4, x]
    yorder = [(y + 2) % 4, (y + 1) % 4, (y + 3) % 4, y]
    swap = [
        send(acc.at[pl.ds((1 - c) * 8 + q * 2, 2)], g_sib.at[q], sib_s.at[i], sib_r.at[i], sib)
        for i, q in enumerate(order)
    ]
    v_swap = send(v.at[pl.ds((1 - c) * 32, 32)], v_sib, sib_s.at[4], sib_r.at[4], sib)
    l_swap = [
        send(
            acc.at[pl.ds(16 + (1 - c) * 32 + q * 8, 8)], l_sib.at[pl.ds(q * 8, 8)],
            sib_s.at[5 + i], sib_r.at[5 + i], sib,
        )
        for i, q in enumerate(order)
    ]

    right, left = at(0, 1), at(0, -1)

    def both(q, j):
        return acc[c * 8 + q * 2 + j] + g_sib[q, j]

    for i in range(3):
        swap[i].wait_recv()
        for j in range(2):
            g_send[i, j] = both(order[i], j)
        if i == 0:
            a2 = send(g_send.at[0, 0], g_two.at[0], gs.at[0], gr.at[0], right)
            b2 = send(g_send.at[0, 1], g_two.at[1], gs.at[1], gr.at[1], left)
        elif i == 1:
            p1 = send(g_send.at[1, 1], g_prev.at[1], gs.at[2], gr.at[2], right)
        else:
            n0 = send(g_send.at[2, 0], g_next.at[0], gs.at[3], gr.at[3], left)
    a2.wait_recv()
    g_send[1, 0] = g_send[1, 0] + g_two[0]
    p0 = send(g_send.at[1, 0], g_prev.at[0], gs.at[4], gr.at[4], right)
    b2.wait_recv()
    g_send[2, 1] = g_send[2, 1] + g_two[1]
    n1 = send(g_send.at[2, 1], g_next.at[1], gs.at[5], gr.at[5], left)
    v_swap.wait_recv()
    split_v(v_sib, 0, 1)
    swap[3].wait_recv()
    for copy in (p1, n0, p0, n1):
        copy.wait_recv()
    for j in range(2):
        update = both(x, j) + g_prev[j] + g_next[j]
        x_own[j] = jnp.dot(
            par_inv[j], par_rhs[j] - update, precision=lax.Precision.HIGHEST, preferred_element_type=F32
        )
    x_swap = send(x_own, x_sib, sib_s.at[9], sib_r.at[9], sib)

    def set_weights(side, ref):
        for j in range(2):
            hi, lo = split(ref[j])
            xw[side, 0, pl.ds(j * BS, BS)] = hi
            xw[side, 1, pl.ds(j * BS, BS)] = lo

    set_weights(0, x_own)
    x_swap.wait_recv()
    set_weights(1, x_sib)

    low = lax.broadcasted_iota(jnp.int32, (BS, BS), 1) < 64

    def products(spots):
        for kx, ky in spots:
            k = kx * 4 + ky
            sums = []
            for j in range(2):
                part = acc[16 + c * 32 + k * 2 + j] + l_sib[k * 2 + j]
                for side in range(2):
                    hi, lo = vh[side, k, j], vl[side, k, j]
                    part = part + (
                        jnp.dot(hi, xw[side, 0], preferred_element_type=F32)
                        + jnp.dot(lo, xw[side, 0], preferred_element_type=F32)
                        + jnp.dot(hi, xw[side, 1], preferred_element_type=F32)
                    )
                sums.append(part)
            for half in range(2):
                first = sums[0][:, half * BS:(half + 1) * BS]
                second = pltpu.roll(sums[1][:, half * BS:(half + 1) * BS], 64, 1)
                for odd in range(2):
                    q = jnp.where(low, second, first) if odd else jnp.where(low, first, second)
                    kz = half * 2 + odd
                    for p, spot in enumerate(((kx, ky, kz), (ky, kz, kx), (kz, kx, ky))):
                        d[p][spot[0], spot[1], spot[2]] = q[ROWS[p][0]:ROWS[p][0] + ROWS[p][1]]

    source = [d, e, f]
    target = [e, f, h]
    first_half, second_half = pl.ds(0, 2), pl.ds(2, 2)
    flying = {(p, ph): [] for p in range(3) for ph in range(3)}

    def place(p, ph):
        axis = (p + ph) % 3
        m = pos[axis]
        return axis, m, source[ph][p], rs_s.at[p, ph], rs_r.at[p, ph]

    def far(p, ph):
        axis, m, src, ss, rr = place(p, ph)
        chunk = src.at[(m + 2) % 4]
        if ph in DIRECT:
            flying[p, ph].append(send(chunk, two[ph][p], ss.at[0], rr.at[0], at(axis, 2)))
        else:
            a, b = first_half, second_half
            flying[p, ph] += [
                send(chunk.at[a], two[ph][p].at[a], ss.at[0], rr.at[0], at(axis, 1)),
                send(chunk.at[b], two[ph][p].at[b], ss.at[1], rr.at[1], at(axis, -1)),
            ]

    def up(p, ph):
        axis, m, src, ss, rr = place(p, ph)
        chunk = src.at[(m + 1) % 4]
        b = second_half
        if ph in DIRECT:
            flying[p, ph].append(send(chunk, prev[ph][p], ss.at[2], rr.at[2], at(axis, 1)))
        else:
            flying[p, ph].append(send(chunk.at[b], prev[ph][p].at[b], ss.at[2], rr.at[2], at(axis, 1)))

    def down(p, ph):
        axis, m, src, ss, rr = place(p, ph)
        chunk = src.at[(m + 3) % 4]
        a = first_half
        if ph in DIRECT:
            flying[p, ph].append(send(chunk, nxt[ph][p], ss.at[3], rr.at[3], at(axis, -1)))
        else:
            flying[p, ph].append(send(chunk.at[a], nxt[ph][p].at[a], ss.at[3], rr.at[3], at(axis, -1)))

    def middle(p, ph):
        if ph in DIRECT:
            return
        axis, m, src, ss, rr = place(p, ph)
        a, b = first_half, second_half
        hi, lo = (m + 1) % 4, (m + 3) % 4
        copies = flying[p, ph]
        copies[0].wait_recv()
        src[hi, a] = src[hi, a] + two[ph][p][a]
        copies.append(send(src.at[hi, a], prev[ph][p].at[a], ss.at[4], rr.at[4], at(axis, 1)))
        copies[1].wait_recv()
        src[lo, b] = src[lo, b] + two[ph][p][b]
        copies.append(send(src.at[lo, b], nxt[ph][p].at[b], ss.at[5], rr.at[5], at(axis, -1)))

    def finish(p, ph):
        axis, m, src, ss, rr = place(p, ph)
        for copy in flying[p, ph] if ph in DIRECT else flying[p, ph][2:]:
            copy.wait_recv()
        got = src[m] + prev[ph][p][...] + nxt[ph][p][...]
        target[ph][p][...] = got + two[ph][p][...] if ph in DIRECT else got

    l_swap[0].wait_recv()
    products([(order[0], q) for q in yorder])
    far(0, 0)
    l_swap[1].wait_recv()
    l_swap[2].wait_recv()
    l_swap[3].wait_recv()
    products([(q, yorder[0]) for q in order[1:]])
    far(1, 0)
    products([(order[1], q) for q in yorder[1:]])
    up(0, 0)
    products([(q, yorder[1]) for q in order[2:]])
    up(1, 0)
    products([(order[2], q) for q in yorder[2:]])
    down(0, 0)
    products([(order[3], q) for q in yorder[2:]])
    down(1, 0)
    far(2, 0)
    up(2, 0)
    down(2, 0)
    for ph in range(3):
        for p in range(3):
            middle(p, ph)
        for p in range(3):
            finish(p, ph)
            if ph < 2:
                far(p, ph + 1)
                up(p, ph + 1)
                down(p, ph + 1)

    for p in range(3):
        total[pl.ds(*ROWS[p])] = h[p][...]
    total[...] = jnp.where(z % 2 == 1, pltpu.roll(total[...], 64, 1), total[...])
    for copy in started:
        copy.wait_send()


def tail_kernel(solved, total, inv, rhs, psol, tsol):
    psol[...] = solved[...]
    turned = total[...].T
    for j in range(2):
        tsol[j] = lax.dot_general(
            rhs[j] - turned[j * 64:(j + 1) * 64], inv[j], (((1,), (1,)), ((), ())),
            precision=lax.Precision.HIGHEST, preferred_element_type=F32,
        )


def leaf_call(*args):
    vm = pl.BlockSpec(memory_space=pltpu.VMEM)
    sm = pl.BlockSpec(memory_space=pltpu.SMEM)
    hb = pl.BlockSpec(memory_space=pl.ANY)
    nl, npar = args[8].shape[0], args[9].shape[0]
    shape = jax.ShapeDtypeStruct
    return pl.pallas_call(
        local_kernel,
        out_shape=(
            pltpu.VMEM((81, BS, NR), F32),
            pltpu.VMEM((64, 2, BS, BS), F32),
        ),
        in_specs=[sm] * 6 + [vm, vm, hb, hb],
        out_specs=(vm, vm),
        scratch_shapes=[
            pltpu.VMEM((4, 3 * BS, NR), BF16),
            pltpu.VMEM((nl, BS, BS), F32),
            pltpu.VMEM((npar, BS, BS), F32),
            pltpu.SemaphoreType.DMA((nl // CH,)),
            pltpu.SemaphoreType.DMA((npar // CH,)),
        ],
        compiler_params=pltpu.CompilerParams(vmem_limit_bytes=36*2**20),
        name="leaf",
    )(*args)


def local(
    leaf_rhs, leaf_inv, par_rhs, par_inv, top_rhs, top_inv, leaf_tiles, leaf_cols, leaf_rows, leaf_count,
    par_tiles, par_cols, par_rows, par_count,
):
    vm = pl.BlockSpec(memory_space=pltpu.VMEM)
    shape = jax.ShapeDtypeStruct
    acc, v = leaf_call(
        leaf_rows, leaf_cols, leaf_count, par_rows, par_cols, par_count,
        leaf_rhs[0], leaf_inv[0], leaf_tiles[0], par_tiles[0],
    )
    n = [r for _, r in ROWS]
    lead = ((4, 4), (4,), ())
    dma = pltpu.SemaphoreType.DMA

    def per_phase():
        return [[pltpu.VMEM(lead[ph] + (r, BS), F32) for r in n] for ph in range(3)]

    block = pltpu.VMEM((2, BS, NR), F32)
    solved, total = pl.pallas_call(
        main_kernel,
        out_shape=(pltpu.VMEM((2, BS, NR), F32), pltpu.VMEM((BS, BS), F32)),
        in_specs=[vm] * 4,
        out_specs=(vm, vm),
        scratch_shapes=[
            pltpu.VMEM((4, 2, BS, NR), F32), pltpu.VMEM((3, 2, BS, NR), F32), block, block, block,
            block, pltpu.VMEM((2, 2, 2 * BS, NR), BF16),
            pltpu.VMEM((32, BS, NR), F32), pltpu.VMEM((32, 2, BS, BS), F32),
            pltpu.VMEM((2, 16, 2, BS, NR), BF16), pltpu.VMEM((2, 16, 2, BS, NR), BF16),
            [pltpu.VMEM((4, 4, 4, r, BS), F32) for r in n],
            [pltpu.VMEM((4, 4, r, BS), F32) for r in n],
            [pltpu.VMEM((4, r, BS), F32) for r in n],
            [pltpu.VMEM((r, BS), F32) for r in n],
            per_phase(), per_phase(), per_phase(),
            dma((10,)), dma((10,)), dma((6,)), dma((6,)), dma((3, 3, 6)), dma((3, 3, 6)),
        ],
        compiler_params=pltpu.CompilerParams(
            collective_id=0, has_side_effects=True, vmem_limit_bytes=36 * 2**20
        ),
        name="main",
    )(
        par_inv[0], par_rhs[0],
        pltpu.with_memory_space_constraint(acc, pltpu.VMEM), pltpu.with_memory_space_constraint(v, pltpu.VMEM),
    )
    psol, tsol = pl.pallas_call(
        tail_kernel,
        out_shape=(shape((2, BS, NR), F32), shape((2, 64, BS), F32)),
        in_specs=[vm] * 4,
        out_specs=(vm, vm),
        name="tail",
    )(
        pltpu.with_memory_space_constraint(solved, pltpu.VMEM),
        pltpu.with_memory_space_constraint(total, pltpu.VMEM),
        top_inv, jnp.swapaxes(top_rhs, 1, 2),
    )
    return psol[None], jnp.swapaxes(tsol, 1, 2)


def solution(mesh):
    four = P("layer", "tile", None, None)
    pair = P("layer", "tile")
    top = P("tile", None, "layer")
    in_specs = (
        four, four, four, four, top, P("tile", None, None), four, pair, pair, pair, four, pair, pair, pair,
    )
    return jax.shard_map(local, mesh=mesh, in_specs=in_specs, out_specs=(four, top), check_vma=False)
```

time: 89.5 us -> 66.7 us (0.75)
  Pallas kernels: 82.4 us -> 64.5 us
  local copies, waits for them, and re-layouts: 4.88 us -> 0 us
    pallas_call x2 -> x3, Pallas kernels: 82.4 us -> 64.5 us  [the longest x1 56.9 us: local(): pl.pallas_call(main_kernel, out_shape=(pltpu.VMEM((2, BS, NR), F32), pltp...]
    unnamed x3 -> x0, local copies, waits for them, and re-layouts: 4.88 us -> none
where the time goes in v2:
time: 66.7 us; the launch traced here: 66.5 us
  Pallas kernels  64.5 us (97%)
  between operations  1.94 us (3%)
    pallas_call x1, Pallas kernels, local(): pl.pallas_call(main_kernel, out_shape=(pltpu.VMEM((2, BS, NR), F32), pltp...  56.9 us
    pallas_call x1, Pallas kernels, leaf_call(): pl.pallas_call(local_kernel, out_shape=(pltpu.VMEM((81, BS, NR), F32), pl...  5.7 us
    pallas_call x1, Pallas kernels, local(): pl.pallas_call(tail_kernel, out_shape=(shape((2, BS, NR), F32), shape((2,...  1.92 us

profile of v2, /device:TPU:0, one launch (start us, length us, event | category | flops | bytes accessed | tf_op | source)
XLA Modules:
  0.0 66.5 jit_solution(7736870206568678515)
XLA Ops:
  1.9 5.7 %leaf.1 = (f32[81,128,256]{2,1,0:T(8,128)S(1)}, f32[64,2,128,128]{3,2,1,0:T(8,128)S(1)}) custom-call(s32[1,160]{1,0:T(1,128)} %lrow.1, s32[1,160]{1,0:T(1,128)} %lcol.1, s32[1,1]{1,0:T(1,128)S(6)} %copy.16.lcnt, s32[1,80]{1,0:T(1,128)} %prow.1, s32[1,80]{1,0:T(1,128)} %pcol.1, s32[1,1]{1,0:T(1,128)S(6)} %copy.17.pcnt, f32[4,128,256]{2,1,0:T(8,128)} %bitcast.11, ...), custom_call_target="tpu_custom_call" | custom-call | tf_op jit(solution)/shard_map/leaf/pallas_call | solution.py:342
  7.6 56.9 %main.1 = (f32[2,128,256]{2,1,0:T(8,128)S(1)}, f32[128,128]{1,0:T(8,128)S(1)}) custom-call(f32[2,128,128]{2,1,0:T(8,128)} %bitcast.14, f32[2,128,256]{2,1,0:T(8,128)} %bitcast.13, f32[81,128,256]{2,1,0:T(8,128)S(1)} %get-tuple-element.8.acc, f32[64,2,128,128]{3,2,1,0:T(8,128)S(1)} %get-tuple-element.9.v), custom_call_target="tpu_custom_call" | custom-call | tf_op jit(solution)/shard_map/main/pallas_call | solution.py:380
  64.6 1.9 %tail.1 = (f32[2,128,256]{2,1,0:T(8,128)}, f32[2,64,128]{2,1,0:T(8,128)}) custom-call(f32[2,128,256]{2,1,0:T(8,128)S(1)} %get-tuple-element.10.solved, f32[128,128]{1,0:T(8,128)S(1)} %get-tuple-element.11.total, f32[2,128,128]{2,1,0:T(8,128)} %inv.1, f32[2,64,128]{2,1,0:T(8,128)} %bitcast.15), custom_call_target="tpu_custom_call" | custom-call | tf_op jit(solution)/shard_map/tail/pallas_call | solution.py:405

commit v3 on v2

v3 whole, which is shorter than its diff:
```python
import jax
import jax.numpy as jnp
from jax import lax
from jax.experimental import pallas as pl
from jax.experimental.pallas import tpu as pltpu
from jax.sharding import PartitionSpec as P

MESH = pl.DeviceIdType.MESH
F32, BF16 = jnp.float32, jnp.bfloat16
BS, NR = 128, 256
CH = 16
UN = 16
PARTS = (
    ((0, 1, 2), 0, 48, 0),
    ((1, 0, 2), 48, 48, 0),
    ((2, 0, 1), 96, 16, None),
    ((0, 1, 2), 0, 48, 1),
    ((1, 0, 2), 48, 48, 1),
    ((2, 1, 0), 112, 16, None),
)
LAST = ((2, 0, 48), (2, 48, 48), (1, 96, 16), (0, 112, 16))
GOES = (0, 1, 2, 0, 1, 3)


def split(t):
    hi = t.astype(BF16)
    return hi, (t - hi.astype(F32)).astype(BF16)


def lhs_cat(t):
    hi, lo = split(t)
    return jnp.concatenate([hi, lo, hi], axis=1)


def rhs_cat(t):
    hi, lo = split(t)
    return jnp.concatenate([hi, hi, lo], axis=0)


def local_kernel(
    lrow, lcol, lcnt, prow, pcol, pcnt, rhs_in, inv_in, ltiles, ptiles,
    acc, vacc,
    xw, rhs, inv, lt, pt, lsem, psem, osem,
):
    nl, npar = lt.shape[0], pt.shape[0]
    count, pcount = lcnt[0, 0], pcnt[0, 0]

    def chunk(src, dst, sem, i):
        return pltpu.make_async_copy(src.at[pl.ds(i * CH, CH)], dst.at[pl.ds(i * CH, CH)], sem.at[i])

    first = (pltpu.make_async_copy(rhs_in, rhs, osem.at[0]), pltpu.make_async_copy(inv_in, inv, osem.at[1]))
    for copy in first:
        copy.start()
    for i in range(nl // CH):
        @pl.when(i * CH < count)
        def _():
            chunk(ltiles, lt, lsem, i).start()
    for i in range(npar // CH):
        @pl.when(i * CH < pcount)
        def _():
            chunk(ptiles, pt, psem, i).start()

    @pl.loop(0, acc.shape[0])
    def _(i):
        acc[i] = jnp.zeros((BS, NR), F32)

    @pl.loop(0, vacc.shape[0])
    def _(i):
        vacc[i] = jnp.zeros((2, BS, BS), F32)

    for copy in first:
        copy.wait()
    for c in range(4):
        x = jnp.dot(inv[c], rhs[c], precision=lax.Precision.HIGHEST, preferred_element_type=F32)
        xw[c] = rhs_cat(x)

    dummy = acc.shape[0] - 1

    def top_place(t):
        return ((t >> 1) & 1) * 32 + (t >> 2) * 2 + (t & 1)

    def group(g, _):
        @pl.when(lax.rem(g, CH // UN) == 0)
        def _():
            chunk(ltiles, lt, lsem, g // (CH // UN)).wait()

        where, prods = [], []
        for u in range(UN):
            s = g * UN + u
            r = lrow[0, s]
            par = ((r >> 1) & 1) * 8 + (r >> 4) * 2 + (r & 1)
            idx = jnp.where(r < 64, par, 16 + top_place(r - 64))
            where.append(jnp.where(s < count, idx, dummy))
            prods.append(jnp.dot(lhs_cat(lt[s]), xw[lcol[0, s]], preferred_element_type=F32))
        for u in range(UN):
            acc[where[u]] += prods[u]
        return 0

    lax.fori_loop(0, (count + UN - 1) // UN, group, 0)
    def dense(s, _):
        @pl.when(lax.rem(s, CH) == 0)
        def _():
            chunk(ptiles, pt, psem, s // CH).wait()

        vacc[top_place(prow[0, s]), pcol[0, s]] += pt[s]
        return 0

    lax.fori_loop(0, pcount, dense, 0)


def main_kernel(
    par_inv_in, par_rhs_in, top_inv_in, top_rhs_in, acc, v,
    x_own, tsol,
    par_inv, par_rhs, top_inv, top_rhs, total,
    g_sib, g_send, g_two, g_prev, g_next, x_sib, xw,
    l_sib, v_sib, vh, vl,
    d, e, f, two, prev, nxt,
    loc, v_sem, sib_s, sib_r, gs, gr, rs_s, rs_r, last_s, last_r,
):
    z = lax.axis_index("layer")
    tile = lax.axis_index("tile")
    x, y, c = tile // 8, (tile // 2) % 4, tile % 2
    pos = (x, y, z)

    def at(axis, step):
        q = [x, y, z]
        q[axis] = (q[axis] + step + 4) % 4
        return (q[2], q[0] * 8 + q[1] * 2 + c)

    sib = (z, x * 8 + y * 2 + 1 - c)
    barrier = pltpu.get_barrier_semaphore()
    peers = [sib] + [at(a, s) for a in range(3) for s in (1, -1, 2)]
    for p in peers:
        pl.semaphore_signal(barrier, inc=1, device_id=p, device_id_type=MESH)

    small = [
        pltpu.make_async_copy(src, dst, loc.at[i])
        for i, (src, dst) in enumerate(
            ((par_inv_in, par_inv), (par_rhs_in, par_rhs), (top_inv_in, top_inv), (top_rhs_in, top_rhs))
        )
    ]
    for copy in small:
        copy.start()

    def split_v(src, base, side):
        @pl.loop(0, 16)
        def _(k):
            for j in range(2):
                for b in range(2):
                    hi, lo = split(src[base + k * 2 + j, b])
                    vh[side, k, j, :, b * BS:(b + 1) * BS] = hi
                    vl[side, k, j, :, b * BS:(b + 1) * BS] = lo

    split_v(v, c * 32, 0)
    pl.semaphore_wait(barrier, len(peers))

    started = []

    def send(src, dst, ssem, rsem, device):
        copy = pltpu.make_async_remote_copy(
            src_ref=src, dst_ref=dst, send_sem=ssem, recv_sem=rsem, device_id=device, device_id_type=MESH
        )
        copy.start()
        started.append(copy)
        return copy

    def leave(*copies):
        for copy in copies:
            copy.wait_send()
            started[:] = [other for other in started if other is not copy]

    order = [(x + 2) % 4, (x + 1) % 4, (x + 3) % 4, x]
    yorder = [(y + 2) % 4, (y + 1) % 4, (y + 3) % 4, y]
    col = (pl.ds(0, BS), pl.ds(BS, BS))

    def swap_g(i, half):
        q = order[i]
        return send(
            acc.at[pl.ds((1 - c) * 8 + q * 2, 2), :, col[half]], g_sib.at[q, :, :, col[half]],
            sib_s.at[half, i], sib_r.at[half, i], sib,
        )

    def swap_l(i, half):
        q = order[i]
        return send(
            acc.at[pl.ds(16 + (1 - c) * 32 + q * 8, 8), :, col[half]], l_sib.at[pl.ds(q * 8, 8), :, col[half]],
            sib_s.at[half, 4 + i], sib_r.at[half, 4 + i], sib,
        )

    right, left = at(0, 1), at(0, -1)
    ring = [{}, {}]

    def gather(i, half):
        swap[half][i].wait_recv()
        q, cut = order[i], col[half]
        for j in range(2):
            g_send[i, j, :, cut] = acc[c * 8 + q * 2 + j, :, cut] + g_sib[q, j, :, cut]

    def hop(half, name, i, src, dst, device):
        cut = col[half]
        ring[half][name] = send(src.at[:, cut], dst.at[:, cut], gs.at[half, i], gr.at[half, i], device)

    def far_g(half):
        hop(half, "a2", 0, g_send.at[0, 0], g_two.at[0], right)
        hop(half, "b2", 1, g_send.at[0, 1], g_two.at[1], left)

    def near_g(half):
        hop(half, "p1", 2, g_send.at[1, 1], g_prev.at[1], right)
        hop(half, "n0", 3, g_send.at[2, 0], g_next.at[0], left)

    def relay_g(half):
        cut = col[half]
        ring[half]["a2"].wait_recv()
        g_send[1, 0, :, cut] = g_send[1, 0, :, cut] + g_two[0, :, cut]
        hop(half, "p0", 4, g_send.at[1, 0], g_prev.at[0], right)
        ring[half]["b2"].wait_recv()
        g_send[2, 1, :, cut] = g_send[2, 1, :, cut] + g_two[1, :, cut]
        hop(half, "n1", 5, g_send.at[2, 1], g_next.at[1], left)

    def solve(half):
        cut = col[half]
        for name in ("p1", "n0", "p0", "n1"):
            ring[half][name].wait_recv()
        for j in range(2):
            known = acc[c * 8 + x * 2 + j, :, cut] + g_sib[x, j, :, cut] + g_prev[j, :, cut] + g_next[j, :, cut]
            x_own[j, :, cut] = jnp.dot(
                par_inv[j], par_rhs[j, :, cut] - known, precision=lax.Precision.HIGHEST, preferred_element_type=F32
            )
        return send(
            x_own.at[:, :, col[half]], x_sib.at[:, :, col[half]], sib_s.at[half, 8], sib_r.at[half, 8], sib
        )

    def set_weights(half, side, ref):
        for j in range(2):
            hi, lo = split(ref[j, :, col[half]])
            xw[half, side, pl.ds(j * BS, BS), col[0]] = hi
            xw[half, side, pl.ds(j * BS, BS), col[1]] = lo

    swap = [[swap_g(0, 0)], []]
    leave(swap[0][0])
    swap[1].append(swap_g(0, 1))
    swap[0] += [swap_g(1, 0), swap_g(2, 0)]
    swap[1] += [swap_g(1, 1), swap_g(2, 1)]
    swap[0].append(swap_g(3, 0))
    swap[1].append(swap_g(3, 1))
    gather(0, 0)
    far_g(0)
    gather(0, 1)
    far_g(1)
    leave(*swap[0][1:3], *swap[1][:3])
    v_swap = send(v.at[pl.ds((1 - c) * 32, 32)], v_sib, v_sem.at[0], v_sem.at[1], sib)
    for half in range(2):
        gather(1, half)
        gather(2, half)
    leave(ring[0]["a2"], ring[0]["b2"])
    near_g(0)
    relay_g(0)
    leave(ring[0]["p0"], ring[0]["n1"])
    near_g(1)
    relay_g(1)
    leave(v_swap)
    l_swap = [[swap_l(i, 0) for i in range(4)], []]
    v_swap.wait_recv()
    split_v(v_sib, 0, 1)
    small[0].wait()
    small[1].wait()
    for half in range(2):
        swap[half][3].wait_recv()
    x_swap = [solve(0)]
    set_weights(0, 0, x_own)
    l_swap[1] += [swap_l(0, 1), swap_l(1, 1)]
    x_swap[0].wait_recv()
    set_weights(0, 1, x_sib)

    low = lax.broadcasted_iota(jnp.int32, (BS, BS), 1) < 64

    def products(half, spots):
        for kx, ky in spots:
            k = kx * 4 + ky
            main, fine = jnp.zeros((2 * BS, NR), F32), jnp.zeros((2 * BS, BS), F32)
            for side in range(2):
                weights = xw[half, side]
                main = main + jnp.dot(
                    vh[side, k].reshape(2 * BS, NR), weights, preferred_element_type=F32
                )
                fine = fine + jnp.dot(
                    vl[side, k].reshape(2 * BS, NR), weights[:, :BS], preferred_element_type=F32
                )
            both = main[:, :BS] + (main[:, BS:] + fine)
            sums = [
                both[j * BS:(j + 1) * BS]
                + (acc[16 + c * 32 + k * 2 + j, :, col[half]] + l_sib[k * 2 + j, :, col[half]])
                for j in range(2)
            ]
            second = pltpu.roll(sums[1], 64, 1)
            for odd in range(2):
                q = jnp.where(low, second, sums[0]) if odd else jnp.where(low, sums[0], second)
                for p, (axes, row, n, of) in enumerate(PARTS):
                    if of not in (None, half):
                        continue
                    spot = (kx, ky, odd if of is not None else half * 2 + odd)
                    s0, s1, s2 = (spot[axis] for axis in axes)
                    d[p][s0, s1, s2] = q[row:row + n]

    front, back = pl.ds(0, 2), pl.ds(2, 2)
    flying = {}

    def place(p):
        axis = PARTS[p][0][0]
        return axis, pos[axis], d[p], rs_s.at[p, 0], rs_r.at[p, 0]

    def far(p):
        axis, m, src, ss, rr = place(p)
        chunk, there = src.at[(m + 2) % 4], two[0][p]
        flying[p, "far"] = [
            send(chunk.at[front], there.at[front], ss.at[0], rr.at[0], at(axis, 1)),
            send(chunk.at[back], there.at[back], ss.at[1], rr.at[1], at(axis, -1)),
        ]

    def near(p):
        axis, m, src, ss, rr = place(p)
        flying[p, "near"] = [
            send(src.at[(m + 1) % 4, back], prev[0][p].at[back], ss.at[2], rr.at[2], at(axis, 1)),
            send(src.at[(m + 3) % 4, front], nxt[0][p].at[front], ss.at[3], rr.at[3], at(axis, -1)),
        ]

    def relay(p):
        axis, m, src, ss, rr = place(p)
        hi, lo = (m + 1) % 4, (m + 3) % 4
        ahead, behind = flying[p, "far"]
        ahead.wait_recv()
        src[hi, front] = src[hi, front] + two[0][p][front]
        one = send(src.at[hi, front], prev[0][p].at[front], ss.at[4], rr.at[4], at(axis, 1))
        behind.wait_recv()
        src[lo, back] = src[lo, back] + two[0][p][back]
        other = send(src.at[lo, back], nxt[0][p].at[back], ss.at[5], rr.at[5], at(axis, -1))
        flying[p, "relay"] = [one, other]

    def straight(key, axis, src, ph, i, ss, rr):
        m = pos[axis]
        flying[key] = [
            send(src.at[(m + step) % 4], there[ph][i], ss.at[k], rr.at[k], at(axis, step))
            for k, (step, there) in enumerate(((2, two), (1, prev), (3, nxt)))
        ]

    def received(key, axis, src, ph, i):
        for copy in flying[key]:
            copy.wait_recv()
        return src[pos[axis]] + prev[ph][i][...] + nxt[ph][i][...] + two[ph][i][...]

    def second_phase(p):
        axis, m, src, ss, rr = place(p)
        for copy in flying[p, "near"] + flying[p, "relay"]:
            copy.wait_recv()
        e[p][...] = src[m] + prev[0][p][...] + nxt[0][p][...]
        straight((p, 1), PARTS[p][0][1], e[p], 1, p, rs_s.at[p, 1], rs_r.at[p, 1])

    def join(p):
        got = received((p, 1), PARTS[p][0][1], e[p], 1, p)
        of = PARTS[p][3]
        if of is None:
            f[GOES[p]][...] = got
        else:
            f[GOES[p]][pl.ds(2 * of, 2)] = got

    def third_phase(i):
        straight((i, 2), LAST[i][0], f[i], 2, i, last_s.at[i], last_r.at[i])

    l_swap[0][0].wait_recv()
    products(0, [(order[0], q) for q in yorder])
    far(0)
    for i in (1, 2, 3):
        l_swap[0][i].wait_recv()
    products(0, [(q, yorder[0]) for q in order[1:]])
    far(1)
    x_swap.append(solve(1))
    l_swap[1] += [swap_l(2, 1), swap_l(3, 1)]
    products(0, [(q, k) for q in order[1:] for k in yorder[1:]])
    near(0)
    near(1)
    set_weights(1, 0, x_own)
    x_swap[1].wait_recv()
    set_weights(1, 1, x_sib)
    l_swap[1][0].wait_recv()
    products(1, [(order[0], q) for q in yorder])
    far(3)
    for i in (1, 2, 3):
        l_swap[1][i].wait_recv()
    products(1, [(q, yorder[0]) for q in order[1:]])
    far(4)
    relay(0)
    relay(1)
    products(1, [(q, k) for q in order[1:] for k in yorder[1:]])
    far(2)
    far(5)
    near(3)
    near(4)
    near(2)
    relay(3)
    relay(4)
    relay(2)
    near(5)
    second_phase(0)
    second_phase(1)
    relay(5)
    for p in (3, 4, 2, 5):
        second_phase(p)
    join(0)
    join(1)
    join(3)
    third_phase(0)
    join(4)
    third_phase(1)
    join(2)
    third_phase(2)
    join(5)
    third_phase(3)
    for i, (axis, row, n) in enumerate(LAST):
        total[pl.ds(row, n)] = received((i, 2), axis, f[i], 2, i)

    turned = jnp.where(z % 2 == 1, pltpu.roll(total[...], 64, 1), total[...]).T
    small[2].wait()
    small[3].wait()
    for j in range(2):
        tsol[j] = lax.dot_general(
            top_rhs[j] - turned[j * 64:(j + 1) * 64], top_inv[j], (((1,), (1,)), ((), ())),
            precision=lax.Precision.HIGHEST, preferred_element_type=F32,
        )
    for copy in started:
        copy.wait_send()


def tail_kernel(solved, top, psol, tsol, sem):
    copies = (pltpu.make_async_copy(solved, psol, sem.at[0]), pltpu.make_async_copy(top, tsol, sem.at[1]))
    for copy in copies:
        copy.start()
    for copy in copies:
        copy.wait()


def leaf_call(*args):
    vm = pl.BlockSpec(memory_space=pltpu.VMEM)
    sm = pl.BlockSpec(memory_space=pltpu.SMEM)
    hb = pl.BlockSpec(memory_space=pl.ANY)
    nl, npar = args[8].shape[0], args[9].shape[0]
    shape = jax.ShapeDtypeStruct
    return pl.pallas_call(
        local_kernel,
        out_shape=(
            pltpu.VMEM((81, BS, NR), F32),
            pltpu.VMEM((64, 2, BS, BS), F32),
        ),
        in_specs=[sm] * 6 + [hb] * 4,
        out_specs=(vm, vm),
        scratch_shapes=[
            pltpu.VMEM((4, 3 * BS, NR), BF16),
            pltpu.VMEM((4, BS, NR), F32),
            pltpu.VMEM((4, BS, BS), F32),
            pltpu.VMEM((nl, BS, BS), F32),
            pltpu.VMEM((npar, BS, BS), F32),
            pltpu.SemaphoreType.DMA((nl // CH,)),
            pltpu.SemaphoreType.DMA((npar // CH,)),
            pltpu.SemaphoreType.DMA((2,)),
        ],
        compiler_params=pltpu.CompilerParams(vmem_limit_bytes=36*2**20),
        name="leaf",
    )(*args)


def local(
    leaf_rhs, leaf_inv, par_rhs, par_inv, top_rhs, top_inv, leaf_tiles, leaf_cols, leaf_rows, leaf_count,
    par_tiles, par_cols, par_rows, par_count,
):
    vm = pl.BlockSpec(memory_space=pltpu.VMEM)
    shape = jax.ShapeDtypeStruct
    acc, v = leaf_call(
        leaf_rows, leaf_cols, leaf_count, par_rows, par_cols, par_count,
        leaf_rhs[0], leaf_inv[0], leaf_tiles[0], par_tiles[0],
    )
    dma = pltpu.SemaphoreType.DMA
    hb = pl.BlockSpec(memory_space=pl.ANY)
    whole = [(4, 4, 4 if of is None else 2, n, BS) for _, _, n, of in PARTS]
    joined = [(4, n, BS) for _, _, n in LAST]
    phases = [[q[1:] for q in whole], [q[2:] for q in whole], [q[1:] for q in joined]]

    def vmem(shapes):
        return [pltpu.VMEM(q, F32) for q in shapes]

    block, square, slim = pltpu.VMEM((2, BS, NR), F32), pltpu.VMEM((2, BS, BS), F32), pltpu.VMEM((2, 64, BS), F32)
    solved, top = pl.pallas_call(
        main_kernel,
        out_shape=(block, slim),
        in_specs=[hb] * 4 + [vm] * 2,
        out_specs=(vm, vm),
        scratch_shapes=[
            square, block, square, slim, pltpu.VMEM((BS, BS), F32),
            pltpu.VMEM((4, 2, BS, NR), F32), pltpu.VMEM((3, 2, BS, NR), F32), block, block, block,
            block, pltpu.VMEM((2, 2, 2 * BS, 2 * BS), BF16),
            pltpu.VMEM((32, BS, NR), F32), pltpu.VMEM((32, 2, BS, BS), F32),
            pltpu.VMEM((2, 16, 2, BS, NR), BF16), pltpu.VMEM((2, 16, 2, BS, NR), BF16),
            vmem(whole), vmem(phases[0]), vmem(joined),
            [vmem(q) for q in phases], [vmem(q) for q in phases], [vmem(q) for q in phases],
            dma((4,)), dma((2,)), dma((2, 9)), dma((2, 9)), dma((2, 6)), dma((2, 6)),
            dma((6, 2, 6)), dma((6, 2, 6)), dma((4, 3)), dma((4, 3)),
        ],
        compiler_params=pltpu.CompilerParams(
            collective_id=0, has_side_effects=True, vmem_limit_bytes=36 * 2**20
        ),
        name="main",
    )(
        par_inv[0], par_rhs[0], top_inv, jnp.swapaxes(top_rhs, 1, 2),
        pltpu.with_memory_space_constraint(acc, pltpu.VMEM), pltpu.with_memory_space_constraint(v, pltpu.VMEM),
    )
    psol, tsol = pl.pallas_call(
        tail_kernel,
        out_shape=(shape((2, BS, NR), F32), shape((2, 64, BS), F32)),
        in_specs=[vm] * 2,
        out_specs=(hb, hb),
        scratch_shapes=[dma((2,))],
        name="tail",
    )(pltpu.with_memory_space_constraint(solved, pltpu.VMEM), pltpu.with_memory_space_constraint(top, pltpu.VMEM))
    return psol[None], jnp.swapaxes(tsol, 1, 2)


def solution(mesh):
    four = P("layer", "tile", None, None)
    pair = P("layer", "tile")
    top = P("tile", None, "layer")
    in_specs = (
        four, four, four, four, top, P("tile", None, None), four, pair, pair, pair, four, pair, pair, pair,
    )
    return jax.shard_map(local, mesh=mesh, in_specs=in_specs, out_specs=(four, top), check_vma=False)
```

time: 66.7 us -> 67 us (level)
    pallas_call x1, Pallas kernels: 5.7 us -> 15.5 us  [leaf_call(): pl.pallas_call(local_kernel, out_shape=(pltpu.VMEM((81, BS, NR), F32), pl...]
    pallas_call x1, Pallas kernels: 56.9 us -> 48.4 us  [local(): pl.pallas_call(main_kernel, out_shape=(block, slim), in_specs=[hb] * 4 +...]
    pallas_call x1, Pallas kernels: 1.92 us -> 0.74 us  [local(): pl.pallas_call(tail_kernel, out_shape=(shape((2, BS, NR), F32), shape((2,...]
where the time goes in v3:
time: 67 us; the launch traced here: 66.6 us
  Pallas kernels  64.6 us (96%)
  between operations  1.94 us (3%)
    pallas_call x1, Pallas kernels, local(): pl.pallas_call(main_kernel, out_shape=(block, slim), in_specs=[hb] * 4 +...  48.4 us
    pallas_call x1, Pallas kernels, leaf_call(): pl.pallas_call(local_kernel, out_shape=(pltpu.VMEM((81, BS, NR), F32), pl...  15.5 us

profile of v3, /device:TPU:0, one launch (start us, length us, event | category | flops | bytes accessed | tf_op | source)
XLA Modules:
  0.0 66.6 jit_solution(12657243262761391151)
XLA Ops:
  1.9 15.5 %leaf.1 = (f32[81,128,256]{2,1,0:T(8,128)S(1)}, f32[64,2,128,128]{3,2,1,0:T(8,128)S(1)}) custom-call(s32[1,160]{1,0:T(1,128)} %lrow.1, s32[1,160]{1,0:T(1,128)} %lcol.1, s32[1,1]{1,0:T(1,128)S(6)} %copy.16.lcnt, s32[1,80]{1,0:T(1,128)} %prow.1, s32[1,80]{1,0:T(1,128)} %pcol.1, s32[1,1]{1,0:T(1,128)S(6)} %copy.17.pcnt, f32[4,128,256]{2,1,0:T(8,128)} %bitcast.11, ...), custom_call_target="tpu_custom_call" | custom-call | tf_op jit(solution)/shard_map/leaf/pallas_call | solution.py:447
  17.4 48.4 %main.1 = (f32[2,128,256]{2,1,0:T(8,128)S(1)}, f32[2,64,128]{2,1,0:T(8,128)S(1)}) custom-call(f32[2,128,128]{2,1,0:T(8,128)} %bitcast.14, f32[2,128,256]{2,1,0:T(8,128)} %bitcast.13, f32[2,128,128]{2,1,0:T(8,128)} %top_inv_in.1, f32[2,64,128]{2,1,0:T(8,128)} %bitcast.15, f32[81,128,256]{2,1,0:T(8,128)S(1)} %get-tuple-element.8.acc, ...), custom_call_target="tpu_custom_call" | custom-call | tf_op jit(solution)/shard_map/main/pallas_call | solution.py:490
  65.8 0.7 %tail.1 = (f32[2,128,256]{2,1,0:T(8,128)}, f32[2,64,128]{2,1,0:T(8,128)}) custom-call(f32[2,128,256]{2,1,0:T(8,128)S(1)} %get-tuple-element.10.solved, f32[2,64,128]{2,1,0:T(8,128)S(1)} %get-tuple-element.11.top), custom_call_target="tpu_custom_call" | custom-call | tf_op jit(solution)/shard_map/tail/pallas_call | solution.py:514

commit v4 on v3

--- a/solution.py
+++ b/solution.py
@@ -27,20 +27,15 @@
     return hi, (t - hi.astype(F32)).astype(BF16)
 
 
-def lhs_cat(t):
-    hi, lo = split(t)
-    return jnp.concatenate([hi, lo, hi], axis=1)
-
-
 def rhs_cat(t):
     hi, lo = split(t)
     return jnp.concatenate([hi, hi, lo], axis=0)
 
 
 def local_kernel(
-    lrow, lcol, lcnt, prow, pcol, pcnt, rhs_in, inv_in, ltiles, ptiles,
+    lrow, lcol, lcnt, prow, pcol, pcnt, rhs, inv, ltiles, ptiles,
     acc, vacc,
-    xw, rhs, inv, lt, pt, lsem, psem, osem,
+    xw, lt, pt, lsem, psem,
 ):
     nl, npar = lt.shape[0], pt.shape[0]
     count, pcount = lcnt[0, 0], pcnt[0, 0]
@@ -48,9 +43,6 @@
     def chunk(src, dst, sem, i):
         return pltpu.make_async_copy(src.at[pl.ds(i * CH, CH)], dst.at[pl.ds(i * CH, CH)], sem.at[i])
 
-    first = (pltpu.make_async_copy(rhs_in, rhs, osem.at[0]), pltpu.make_async_copy(inv_in, inv, osem.at[1]))
-    for copy in first:
-        copy.start()
     for i in range(nl // CH):
         @pl.when(i * CH < count)
         def _():
@@ -68,13 +60,11 @@
     def _(i):
         vacc[i] = jnp.zeros((2, BS, BS), F32)
 
-    for copy in first:
-        copy.wait()
     for c in range(4):
         x = jnp.dot(inv[c], rhs[c], precision=lax.Precision.HIGHEST, preferred_element_type=F32)
         xw[c] = rhs_cat(x)
 
-    dummy = acc.shape[0] - 1
+    dummy, vdummy = acc.shape[0] - 1, vacc.shape[0] - 1
 
     def top_place(t):
         return ((t >> 1) & 1) * 32 + (t >> 2) * 2 + (t & 1)
@@ -91,21 +81,28 @@
             par = ((r >> 1) & 1) * 8 + (r >> 4) * 2 + (r & 1)
             idx = jnp.where(r < 64, par, 16 + top_place(r - 64))
             where.append(jnp.where(s < count, idx, dummy))
-            prods.append(jnp.dot(lhs_cat(lt[s]), xw[lcol[0, s]], preferred_element_type=F32))
+            hi, lo = split(lt[s])
+            w = xw[lcol[0, s]]
+            prods.append(
+                jnp.dot(jnp.concatenate([hi, lo], axis=1), w[:2 * BS], preferred_element_type=F32)
+                + jnp.dot(hi, w[2 * BS:], preferred_element_type=F32)
+            )
         for u in range(UN):
             acc[where[u]] += prods[u]
         return 0
 
     lax.fori_loop(0, (count + UN - 1) // UN, group, 0)
-    def dense(s, _):
-        @pl.when(lax.rem(s, CH) == 0)
+    def dense(g, _):
+        @pl.when(lax.rem(g, CH // 4) == 0)
         def _():
-            chunk(ptiles, pt, psem, s // CH).wait()
-
-        vacc[top_place(prow[0, s]), pcol[0, s]] += pt[s]
+            chunk(ptiles, pt, psem, g // (CH // 4)).wait()
+
+        for u in range(4):
+            s = g * 4 + u
+            vacc[jnp.where(s < pcount, top_place(prow[0, s]), vdummy), pcol[0, s]] += pt[s]
         return 0
 
-    lax.fori_loop(0, pcount, dense, 0)
+    lax.fori_loop(0, (pcount + 3) // 4, dense, 0)
 
 
 def main_kernel(
@@ -236,30 +233,25 @@
             xw[half, side, pl.ds(j * BS, BS), col[0]] = hi
             xw[half, side, pl.ds(j * BS, BS), col[1]] = lo
 
-    swap = [[swap_g(0, 0)], []]
-    leave(swap[0][0])
-    swap[1].append(swap_g(0, 1))
-    swap[0] += [swap_g(1, 0), swap_g(2, 0)]
-    swap[1] += [swap_g(1, 1), swap_g(2, 1)]
-    swap[0].append(swap_g(3, 0))
-    swap[1].append(swap_g(3, 1))
+    swap = [[swap_g(0, 0)], [swap_g(0, 1)]]
+    leave(swap[0][0], swap[1][0])
+    for i in (1, 2, 3):
+        for half in range(2):
+            swap[half].append(swap_g(i, half))
+    v_swap = send(v.at[pl.ds((1 - c) * 32, 32)], v_sib, v_sem.at[0], v_sem.at[1], sib)
     gather(0, 0)
     far_g(0)
     gather(0, 1)
     far_g(1)
-    leave(*swap[0][1:3], *swap[1][:3])
-    v_swap = send(v.at[pl.ds((1 - c) * 32, 32)], v_sib, v_sem.at[0], v_sem.at[1], sib)
     for half in range(2):
         gather(1, half)
         gather(2, half)
     leave(ring[0]["a2"], ring[0]["b2"])
     near_g(0)
+    near_g(1)
     relay_g(0)
-    leave(ring[0]["p0"], ring[0]["n1"])
-    near_g(1)
+    l_swap = [[swap_l(i, 0) for i in range(4)], []]
     relay_g(1)
-    leave(v_swap)
-    l_swap = [[swap_l(i, 0) for i in range(4)], []]
     v_swap.wait_recv()
     split_v(v_sib, 0, 1)
     small[0].wait()
@@ -268,7 +260,7 @@
         swap[half][3].wait_recv()
     x_swap = [solve(0)]
     set_weights(0, 0, x_own)
-    l_swap[1] += [swap_l(0, 1), swap_l(1, 1)]
+    l_swap[1] += [swap_l(i, 1) for i in range(4)]
     x_swap[0].wait_recv()
     set_weights(0, 1, x_sib)
 
@@ -374,7 +366,6 @@
     products(0, [(q, yorder[0]) for q in order[1:]])
     far(1)
     x_swap.append(solve(1))
-    l_swap[1] += [swap_l(2, 1), swap_l(3, 1)]
     products(0, [(q, k) for q in order[1:] for k in yorder[1:]])
     near(0)
     near(1)
@@ -448,19 +439,16 @@
         local_kernel,
         out_shape=(
             pltpu.VMEM((81, BS, NR), F32),
-            pltpu.VMEM((64, 2, BS, BS), F32),
+            pltpu.VMEM((65, 2, BS, BS), F32),
         ),
-        in_specs=[sm] * 6 + [hb] * 4,
+        in_specs=[sm] * 6 + [vm, vm, hb, hb],
         out_specs=(vm, vm),
         scratch_shapes=[
             pltpu.VMEM((4, 3 * BS, NR), BF16),
-            pltpu.VMEM((4, BS, NR), F32),
-            pltpu.VMEM((4, BS, BS), F32),
             pltpu.VMEM((nl, BS, BS), F32),
             pltpu.VMEM((npar, BS, BS), F32),
             pltpu.SemaphoreType.DMA((nl // CH,)),
             pltpu.SemaphoreType.DMA((npar // CH,)),
-            pltpu.SemaphoreType.DMA((2,)),
         ],
         compiler_params=pltpu.CompilerParams(vmem_limit_bytes=36*2**20),
         name="leaf",

time: 67 us -> 62.2 us (0.928)
  Pallas kernels: 64.6 us -> 59.8 us
    pallas_call x1, Pallas kernels: 15.5 us -> 7.14 us  [leaf_call(): pl.pallas_call(local_kernel, out_shape=(pltpu.VMEM((81, BS, NR), F32), pl...]
    pallas_call x1, Pallas kernels: 48.4 us -> 52 us  [local(): pl.pallas_call(main_kernel, out_shape=(block, slim), in_specs=[hb] * 4 +...]
where the time goes in v4:
time: 62.2 us; the launch traced here: 61.8 us
  Pallas kernels  59.8 us (96%)
  between operations  1.94 us (3%)
    pallas_call x1, Pallas kernels, local(): pl.pallas_call(main_kernel, out_shape=(block, slim), in_specs=[hb] * 4 +...  52 us
    pallas_call x1, Pallas kernels, leaf_call(): pl.pallas_call(local_kernel, out_shape=(pltpu.VMEM((81, BS, NR), F32), pl...  7.14 us

profile of v4, /device:TPU:0, one launch (start us, length us, event | category | flops | bytes accessed | tf_op | source)
XLA Modules:
  0.0 61.8 jit_solution(12553195781844817253)
XLA Ops:
  1.9 7.1 %leaf.1 = (f32[81,128,256]{2,1,0:T(8,128)S(1)}, f32[65,2,128,128]{3,2,1,0:T(8,128)S(1)}) custom-call(s32[1,160]{1,0:T(1,128)} %lrow.1, s32[1,160]{1,0:T(1,128)} %lcol.1, s32[1,1]{1,0:T(1,128)S(6)} %copy.16.lcnt, s32[1,80]{1,0:T(1,128)} %prow.1, s32[1,80]{1,0:T(1,128)} %pcol.1, s32[1,1]{1,0:T(1,128)S(6)} %copy.17.pcnt, f32[4,128,256]{2,1,0:T(8,128)} %bitcast.11, ...), custom_call_target="tpu_custom_call" | custom-call | tf_op jit(solution)/shard_map/leaf/pallas_call | solution.py:438
  9.1 52.0 %main.1 = (f32[2,128,256]{2,1,0:T(8,128)S(1)}, f32[2,64,128]{2,1,0:T(8,128)S(1)}) custom-call(f32[2,128,128]{2,1,0:T(8,128)} %bitcast.14, f32[2,128,256]{2,1,0:T(8,128)} %bitcast.13, f32[2,128,128]{2,1,0:T(8,128)} %top_inv_in.1, f32[2,64,128]{2,1,0:T(8,128)} %bitcast.15, f32[81,128,256]{2,1,0:T(8,128)S(1)} %get-tuple-element.8.acc, ...), custom_call_target="tpu_custom_call" | custom-call | tf_op jit(solution)/shard_map/main/pallas_call | solution.py:478
  61.0 0.7 %tail.1 = (f32[2,128,256]{2,1,0:T(8,128)}, f32[2,64,128]{2,1,0:T(8,128)}) custom-call(f32[2,128,256]{2,1,0:T(8,128)S(1)} %get-tuple-element.10.solved, f32[2,64,128]{2,1,0:T(8,128)S(1)} %get-tuple-element.11.top), custom_call_target="tpu_custom_call" | custom-call | tf_op jit(solution)/shard_map/tail/pallas_call | solution.py:502

commit v5 on v4

--- a/solution.py
+++ b/solution.py
@@ -9,7 +9,7 @@
 F32, BF16 = jnp.float32, jnp.bfloat16
 BS, NR = 128, 256
 CH = 16
-UN = 16
+UN = 32
 PARTS = (
     ((0, 1, 2), 0, 48, 0),
     ((1, 0, 2), 48, 48, 0),
@@ -70,9 +70,10 @@
         return ((t >> 1) & 1) * 32 + (t >> 2) * 2 + (t & 1)
 
     def group(g, _):
-        @pl.when(lax.rem(g, CH // UN) == 0)
-        def _():
-            chunk(ltiles, lt, lsem, g // (CH // UN)).wait()
+        for i in range(UN // CH):
+            @pl.when((g * (UN // CH) + i) * CH < count)
+            def _():
+                chunk(ltiles, lt, lsem, g * (UN // CH) + i).wait()
 
         where, prods = [], []
         for u in range(UN):

time: 62.2 us -> 62.3 us (level)
    pallas_call x1, Pallas kernels: 7.14 us -> 9.9 us  [leaf_call(): pl.pallas_call(local_kernel, out_shape=(pltpu.VMEM((81, BS, NR), F32), pl...]
    pallas_call x1, Pallas kernels: 52 us -> 49.3 us  [local(): pl.pallas_call(main_kernel, out_shape=(block, slim), in_specs=[hb] * 4 +...]
where the time goes in v5:
time: 62.3 us; the launch traced here: 61.9 us
  Pallas kernels  59.9 us (96%)
  between operations  1.94 us (3%)
    pallas_call x1, Pallas kernels, local(): pl.pallas_call(main_kernel, out_shape=(block, slim), in_specs=[hb] * 4 +...  49.3 us
    pallas_call x1, Pallas kernels, leaf_call(): pl.pallas_call(local_kernel, out_shape=(pltpu.VMEM((81, BS, NR), F32), pl...  9.9 us

profile of v5, /device:TPU:0, one launch (start us, length us, event | category | flops | bytes accessed | tf_op | source)
XLA Modules:
  0.0 61.9 jit_solution(14459209378602299846)
XLA Ops:
  1.9 9.9 %leaf.1 = (f32[81,128,256]{2,1,0:T(8,128)S(1)}, f32[65,2,128,128]{3,2,1,0:T(8,128)S(1)}) custom-call(s32[1,160]{1,0:T(1,128)} %lrow.1, s32[1,160]{1,0:T(1,128)} %lcol.1, s32[1,1]{1,0:T(1,128)S(6)} %copy.16.lcnt, s32[1,80]{1,0:T(1,128)} %prow.1, s32[1,80]{1,0:T(1,128)} %pcol.1, s32[1,1]{1,0:T(1,128)S(6)} %copy.17.pcnt, f32[4,128,256]{2,1,0:T(8,128)} %bitcast.11, ...), custom_call_target="tpu_custom_call" | custom-call | tf_op jit(solution)/shard_map/leaf/pallas_call | solution.py:439
  11.8 49.3 %main.1 = (f32[2,128,256]{2,1,0:T(8,128)S(1)}, f32[2,64,128]{2,1,0:T(8,128)S(1)}) custom-call(f32[2,128,128]{2,1,0:T(8,128)} %bitcast.14, f32[2,128,256]{2,1,0:T(8,128)} %bitcast.13, f32[2,128,128]{2,1,0:T(8,128)} %top_inv_in.1, f32[2,64,128]{2,1,0:T(8,128)} %bitcast.15, f32[81,128,256]{2,1,0:T(8,128)S(1)} %get-tuple-element.8.acc, ...), custom_call_target="tpu_custom_call" | custom-call | tf_op jit(solution)/shard_map/main/pallas_call | solution.py:479
  61.2 0.7 %tail.1 = (f32[2,128,256]{2,1,0:T(8,128)}, f32[2,64,128]{2,1,0:T(8,128)}) custom-call(f32[2,128,256]{2,1,0:T(8,128)S(1)} %get-tuple-element.10.solved, f32[2,64,128]{2,1,0:T(8,128)S(1)} %get-tuple-element.11.top), custom_call_target="tpu_custom_call" | custom-call | tf_op jit(solution)/shard_map/tail/pallas_call | solution.py:503

commit v6 on v5

--- a/solution.py
+++ b/solution.py
@@ -367,9 +367,11 @@
     products(0, [(q, yorder[0]) for q in order[1:]])
     far(1)
     x_swap.append(solve(1))
-    products(0, [(q, k) for q in order[1:] for k in yorder[1:]])
+    products(0, [(q, k) for q in order[1:3] for k in yorder[1:]])
     near(0)
+    products(0, [(order[3], k) for k in yorder[1:3]])
     near(1)
+    products(0, [(order[3], yorder[3])])
     set_weights(1, 0, x_own)
     x_swap[1].wait_recv()
     set_weights(1, 1, x_sib)

time: 62.3 us -> 62.3 us (level)
    pallas_call x1, Pallas kernels: 9.9 us -> 7.61 us  [leaf_call(): pl.pallas_call(local_kernel, out_shape=(pltpu.VMEM((81, BS, NR), F32), pl...]
    pallas_call x1, Pallas kernels: 49.3 us -> 51 us  [local(): pl.pallas_call(main_kernel, out_shape=(block, slim), in_specs=[hb] * 4 +...]
where the time goes in v6:
time: 62.3 us; the launch traced here: 61.3 us
  Pallas kernels  59.4 us (95%)
  between operations  1.94 us (3%)
    pallas_call x1, Pallas kernels, local(): pl.pallas_call(main_kernel, out_shape=(block, slim), in_specs=[hb] * 4 +...  51 us
    pallas_call x1, Pallas kernels, leaf_call(): pl.pallas_call(local_kernel, out_shape=(pltpu.VMEM((81, BS, NR), F32), pl...  7.61 us

profile of v6, /device:TPU:0, one launch (start us, length us, event | category | flops | bytes accessed | tf_op | source)
XLA Modules:
  0.0 61.3 jit_solution(8452331872610724340)
XLA Ops:
  1.9 7.6 %leaf.1 = (f32[81,128,256]{2,1,0:T(8,128)S(1)}, f32[65,2,128,128]{3,2,1,0:T(8,128)S(1)}) custom-call(s32[1,160]{1,0:T(1,128)} %lrow.1, s32[1,160]{1,0:T(1,128)} %lcol.1, s32[1,1]{1,0:T(1,128)S(6)} %copy.16.lcnt, s32[1,80]{1,0:T(1,128)} %prow.1, s32[1,80]{1,0:T(1,128)} %pcol.1, s32[1,1]{1,0:T(1,128)S(6)} %copy.17.pcnt, f32[4,128,256]{2,1,0:T(8,128)} %bitcast.11, ...), custom_call_target="tpu_custom_call" | custom-call | tf_op jit(solution)/shard_map/leaf/pallas_call | solution.py:441
  9.5 51.0 %main.1 = (f32[2,128,256]{2,1,0:T(8,128)S(1)}, f32[2,64,128]{2,1,0:T(8,128)S(1)}) custom-call(f32[2,128,128]{2,1,0:T(8,128)} %bitcast.14, f32[2,128,256]{2,1,0:T(8,128)} %bitcast.13, f32[2,128,128]{2,1,0:T(8,128)} %top_inv_in.1, f32[2,64,128]{2,1,0:T(8,128)} %bitcast.15, f32[81,128,256]{2,1,0:T(8,128)S(1)} %get-tuple-element.8.acc, ...), custom_call_target="tpu_custom_call" | custom-call | tf_op jit(solution)/shard_map/main/pallas_call | solution.py:481
  60.6 0.7 %tail.1 = (f32[2,128,256]{2,1,0:T(8,128)}, f32[2,64,128]{2,1,0:T(8,128)}) custom-call(f32[2,128,256]{2,1,0:T(8,128)S(1)} %get-tuple-element.10.solved, f32[2,64,128]{2,1,0:T(8,128)S(1)} %get-tuple-element.11.top), custom_call_target="tpu_custom_call" | custom-call | tf_op jit(solution)/shard_map/tail/pallas_call | solution.py:505
